TPU v7x, 256 devices: a whole 4x4x8 slice. The times are simulated.
256 devices in a mesh: grp: 4 (over y), blk: 64 (over z, x, core).
Axes of the slice: x: 4, y: 4, z: 8, core: 2. Of those that a mesh axis runs over, the one named last changes fastest.
Arguments:
- rhs: bfloat16 [1, 768, 4096], P(None, 'blk', 'grp'), may hold values from -6 to 6
- lower_factor_tiles: bfloat16 [1, 32768, 1024], P(None, ('grp', 'blk')), may hold values from -0.09375 to 0.09375
- tile_rows: int32 [1, 4, 128], P(None, 'grp'), may hold values from 16 to 192, as said below
- diag_inv: bfloat16 [1, 4096, 512], P(None, 'grp'), as said below
- inner_block: bfloat16 [1, 2048, 512], P(None, 'grp'), may hold values from -0.1875 to 0.1875
- lower_row_solution: bfloat16 [768, 8192], P('blk'), may hold values from -6 to 6
Outputs:
- forward_solution: bfloat16 [1, 768, 4096], P(None, 'blk', 'grp')
- pending_lower_updates: float32 [768, 8192], P('blk', 'grp')
- solution: bfloat16 [1, 768, 4096], P(None, 'blk', 'grp')
Inputs may be any that keep to these rules, and one draw needn't show every extreme that they name: tile_rows[r, g] gives for each of the 128 slots of panel p = r * 4 + g a row tile below that panel, at least (p + 1) * 16, or 192 for an empty slot; no row tile appears twice in one panel. `diag_inv`: each 512 x 512 block is upper triangular.
All inputs are finite; a program needn't handle non-finite values.
Results may differ from a plain program's by a relative error of at most 0.0085.
Values may be sent and summed in bfloat16 or wider, within the bound.
No kernel may reach another device: no remote copies, remote signals or barrier semaphores. Data moves between devices by JAX's collectives and lax.ppermute only.
A program may use at most 64 MiB of HBM per device.

v0:
```python
import jax
import jax.numpy as jnp
from jax import lax
from jax.sharding import PartitionSpec as P

TILE_HEIGHT = 64


def shifted(x, axis, by):
    count = lax.axis_size(axis)
    return lax.ppermute(x, axis, [(i, (i + by) % count) for i in range(count)])


def lower_solve(residue, inverse, coupling):
    highest = lax.Precision.HIGHEST
    split_at = inverse.shape[1]
    leading = jnp.dot(
        residue[:, :split_at], inverse[:split_at].astype(jnp.float32), precision=highest
    ).astype(jnp.bfloat16)
    leading_kept = lax.optimization_barrier(leading)
    carried = residue[:, split_at:] - jnp.dot(
        leading_kept.astype(jnp.float32), coupling.astype(jnp.float32), precision=highest
    )
    second = jnp.dot(carried, inverse[split_at:].astype(jnp.float32), precision=highest).astype(
        jnp.bfloat16
    )
    return jnp.concatenate([leading, second], axis=1)


def upper_solve(residue, inverse, coupling):
    highest = lax.Precision.HIGHEST
    split_at = inverse.shape[1]
    contract = (((1,), (1,)), ((), ()))
    second = lax.dot_general(
        residue[:, split_at:], inverse[split_at:].astype(jnp.float32), contract, precision=highest
    ).astype(jnp.bfloat16)
    second_kept = lax.optimization_barrier(second)
    carried = residue[:, :split_at] - lax.dot_general(
        second_kept.astype(jnp.float32), coupling.astype(jnp.float32), contract, precision=highest
    )
    leading = lax.dot_general(
        carried, inverse[:split_at].astype(jnp.float32), contract, precision=highest
    ).astype(jnp.bfloat16)
    return jnp.concatenate([leading, second], axis=1)


def body(rhs, lower_factor_tiles, tile_rows, diag_inv, inner_block, lower_row_solution):
    rounds, local_cases, panel_width = rhs.shape
    groups = lax.axis_size("grp")
    devices = lax.axis_size("blk")
    group_index = lax.axis_index("grp")
    total_panel_count = rounds * groups
    slot_table = tile_rows[:, 0, :]
    slot_count = slot_table.shape[1]
    slot_height = lower_factor_tiles.shape[1]
    tiles_per_panel = panel_width // TILE_HEIGHT
    tile_total = total_panel_count * tiles_per_panel
    full_total = tile_total + slot_count
    block_count = 1
    block_cases = local_cases // block_count
    step_count = total_panel_count + block_count - 1

    def relay_state(moving, offset):
        return shifted(moving, "grp", offset)

    def panel_inputs(clamped):
        panel_round_index = clamped // groups
        tile_collection = lax.dynamic_index_in_dim(lower_factor_tiles, panel_round_index, 0, False)
        row_numbers = lax.dynamic_index_in_dim(slot_table, panel_round_index, 0, False)
        inverse = lax.dynamic_index_in_dim(diag_inv, panel_round_index, 0, False)
        coupling = lax.dynamic_index_in_dim(inner_block, panel_round_index, 0, False)
        return (tile_collection, row_numbers, inverse, coupling, panel_round_index)

    def forward_step(step_index, loop_state):
        outstanding_updates, forward_out = loop_state
        case_block = (step_index - group_index) % block_count
        panel_index = step_index - case_block
        active_flag = (
            (panel_index >= 0)
            & (panel_index < total_panel_count)
            & (panel_index % groups == group_index)
        )
        clamped = jnp.clip(panel_index, 0, total_panel_count - 1)
        tile_collection, row_numbers, inverse, coupling, panel_round_index = panel_inputs(clamped)
        outstanding_updates = jnp.where(
            panel_index == 0, jnp.zeros_like(outstanding_updates), outstanding_updates
        )
        given_rhs = rhs[0]
        owed_rows = lax.dynamic_slice_in_dim(
            outstanding_updates, clamped * tiles_per_panel, tiles_per_panel, 1
        ).reshape(block_cases, panel_width)
        solved = lower_solve(given_rhs.astype(jnp.float32) - owed_rows, inverse, coupling)
        solved = jnp.where(active_flag, solved, jnp.zeros_like(solved))
        products = lax.dot_general(
            lax.all_gather(solved, "blk", axis=0, tiled=True),
            tile_collection,
            (((1,), (1,)), ((), ())),
            preferred_element_type=jnp.float32,
        )
        arrived = lax.all_to_all(products, "blk", split_axis=0, concat_axis=1, tiled=True)
        outstanding_updates = outstanding_updates.at[:, row_numbers, :].add(
            arrived.reshape(block_cases, slot_count, TILE_HEIGHT)
        )
        earlier = forward_out
        forward_out = jnp.where(active_flag, solved[None], earlier)
        return (relay_state(outstanding_updates, 1), forward_out)

    outstanding_updates = jnp.zeros((block_cases, full_total + 1, TILE_HEIGHT), jnp.float32)
    forward_out = jnp.zeros((rounds, local_cases, panel_width), jnp.bfloat16)
    outstanding_updates, forward_out = lax.fori_loop(
        0, step_count, forward_step, (outstanding_updates, forward_out)
    )
    beyond = outstanding_updates[:, tile_total:full_total, :].reshape(
        block_cases, slot_count * TILE_HEIGHT
    )
    is_holder = (block_count > 1) | (group_index == 0)
    beyond = jnp.where(is_holder, beyond, jnp.zeros_like(beyond))
    pending_lower_updates = lax.psum_scatter(
        beyond.astype(jnp.bfloat16), "grp", scatter_dimension=1, tiled=True
    ).astype(jnp.float32)

    def backward_step(step_index, loop_state):
        finished_rows, solution_out = loop_state
        case_block = (step_index - (total_panel_count - 1 - group_index)) % block_count
        chain_depth = step_index - case_block
        panel_index = total_panel_count - 1 - chain_depth
        active_flag = (
            (chain_depth >= 0)
            & (chain_depth < total_panel_count)
            & (panel_index % groups == group_index)
        )
        clamped = jnp.clip(panel_index, 0, total_panel_count - 1)
        tile_collection, row_numbers, inverse, coupling, panel_round_index = panel_inputs(clamped)
        root_rows = lower_row_solution.astype(jnp.float32)
        initial = jnp.concatenate(
            [
                jnp.zeros((block_cases, tile_total, TILE_HEIGHT), jnp.float32),
                root_rows.reshape(block_cases, slot_count, TILE_HEIGHT),
                jnp.zeros((block_cases, 1, TILE_HEIGHT), jnp.float32),
            ],
            axis=1,
        )
        finished_rows = jnp.where(chain_depth == 0, initial, finished_rows)
        selected_rows = (
            finished_rows[:, row_numbers, :]
            .astype(jnp.bfloat16)
            .reshape(block_cases, devices, slot_height)
        )
        received = lax.all_to_all(
            selected_rows, "blk", split_axis=1, concat_axis=0, tiled=True
        ).reshape(devices * block_cases, slot_height)
        transposed = lax.psum_scatter(
            jnp.dot(received, tile_collection, preferred_element_type=jnp.float32),
            "blk",
            scatter_dimension=0,
            tiled=True,
        )
        forward_part = forward_out[0]
        solved = upper_solve(forward_part.astype(jnp.float32) - transposed, inverse, coupling)
        solved = jnp.where(active_flag, solved, jnp.zeros_like(solved))
        finished_rows = lax.dynamic_update_slice_in_dim(
            finished_rows,
            solved.astype(jnp.float32).reshape(block_cases, tiles_per_panel, TILE_HEIGHT),
            clamped * tiles_per_panel,
            1,
        )
        earlier = solution_out
        solution_out = jnp.where(active_flag, solved[None], earlier)
        return (relay_state(finished_rows, -1), solution_out)

    finished_rows = jnp.zeros((block_cases, full_total + 1, TILE_HEIGHT), jnp.float32)
    solution_out = jnp.zeros((rounds, local_cases, panel_width), jnp.bfloat16)
    finished_rows, solution_out = lax.fori_loop(
        0, step_count, backward_step, (finished_rows, solution_out)
    )
    return (forward_out, pending_lower_updates, solution_out)


def solution(mesh):
    placed = (
        P(None, "blk", "grp"),
        P(None, ("grp", "blk"), None),
        P(None, "grp", None),
        P(None, "grp", None),
        P(None, "grp", None),
        P("blk", None),
    )
    return jax.shard_map(
        body,
        mesh=mesh,
        in_specs=placed,
        out_specs=(P(None, "blk", "grp"), P("blk", "grp"), P(None, "blk", "grp")),
        check_vma=False,
    )
```

profile of v0, /device:TPU:16, one launch (start us, length us, event | category | flops | bytes accessed | tf_op | source)
XLA Modules:
  0.0 1224.6 jit_solution(15095761955985604609)
XLA Ops:
  8.1 543.6 %while.37 = (s32[]{:T(128)}, f32[12,193,64]{1,2,0:T(8,128)S(1)}, bf16[1,12,1024]{2,1,0:T(8,128)(2,1)}, s32[1,128]{1,0:T(1,128)}, s32[]{:T(128)}, /*index=5*/bf16...) while((s32[]{:T(128)}, f32[12,193,64]{1,2,0:T(8,128)S(1)}, ...), condition=%wide.region_2.3_spmd.clone, body=%wide.region_0.2_spmd.clone.sunk | while | flops 283552896 | bytes 26859540 | solution.py:110
  13.5 80.1 %all-gather.6.cloned.1.call-done = bf16[64,12,1024]{2,1,0:T(8,128)(2,1)} async-done(((bf16[1,12,1024]{2,1,0:T(8,128)(2,1)}), bf16[64,12,1024]{2,1,0:T(8,128)(2,1)}) %all-gather.6.cloned.1.call-update) | async-done | bytes 1572880 | tf_op jit(solution)/shard_map/while/body/eval_jaxpr/all_gather | solution.py:95
  105.0 17.6 %all-to-all-done = f32[64,12,128]{2,1,0:T(8,128)S(1)} async-done(((f32[64,12,128]{2,1,0:T(8,128)}), f32[64,12,128]{2,1,0:T(8,128)S(1)}, u32[]{:S(2)}, u32[]{:S(2)}) %all-to-all-start) | async-done | bytes 393248 | tf_op jit(solution)/shard_map/while/body/eval_jaxpr/all_to_all | solution.py:100
  131.2 17.7 %collective-permute-done = f32[12,193,64]{1,2,0:T(8,128)S(1)} collective-permute-done((f32[12,193,64]{1,2,0:T(8,128)S(1)}, f32[12,193,64]{1,2,0:T(8,128)S(1)}, u32[]{:S(2)}, u32[]{:S(2)}) %collective-permute-start) | collective-permute-done | bytes 592928 | tf_op jit(solution)/shard_map/while/body/eval_jaxpr/ppermute | solution.py:11
  154.3 73.6 %all-gather.6.cloned.1.call-done = bf16[64,12,1024]{2,1,0:T(8,128)(2,1)} async-done(((bf16[1,12,1024]{2,1,0:T(8,128)(2,1)}), bf16[64,12,1024]{2,1,0:T(8,128)(2,1)}) %all-gather.6.cloned.1.call-update) | async-done | bytes 1572880 | tf_op jit(solution)/shard_map/while/body/eval_jaxpr/all_gather | solution.py:95
  239.3 17.6 %all-to-all-done = f32[64,12,128]{2,1,0:T(8,128)S(1)} async-done(((f32[64,12,128]{2,1,0:T(8,128)}), f32[64,12,128]{2,1,0:T(8,128)S(1)}, u32[]{:S(2)}, u32[]{:S(2)}) %all-to-all-start) | async-done | bytes 393248 | tf_op jit(solution)/shard_map/while/body/eval_jaxpr/all_to_all | solution.py:100
  266.2 17.0 %collective-permute-done = f32[12,193,64]{1,2,0:T(8,128)S(1)} collective-permute-done((f32[12,193,64]{1,2,0:T(8,128)S(1)}, f32[12,193,64]{1,2,0:T(8,128)S(1)}, u32[]{:S(2)}, u32[]{:S(2)}) %collective-permute-start) | collective-permute-done | bytes 592928 | tf_op jit(solution)/shard_map/while/body/eval_jaxpr/ppermute | solution.py:11
  288.6 73.6 %all-gather.6.cloned.1.call-done = bf16[64,12,1024]{2,1,0:T(8,128)(2,1)} async-done(((bf16[1,12,1024]{2,1,0:T(8,128)(2,1)}), bf16[64,12,1024]{2,1,0:T(8,128)(2,1)}) %all-gather.6.cloned.1.call-update) | async-done | bytes 1572880 | tf_op jit(solution)/shard_map/while/body/eval_jaxpr/all_gather | solution.py:95
  373.5 17.6 %all-to-all-done = f32[64,12,128]{2,1,0:T(8,128)S(1)} async-done(((f32[64,12,128]{2,1,0:T(8,128)}), f32[64,12,128]{2,1,0:T(8,128)S(1)}, u32[]{:S(2)}, u32[]{:S(2)}) %all-to-all-start) | async-done | bytes 393248 | tf_op jit(solution)/shard_map/while/body/eval_jaxpr/all_to_all | solution.py:100
  400.4 17.0 %collective-permute-done = f32[12,193,64]{1,2,0:T(8,128)S(1)} collective-permute-done((f32[12,193,64]{1,2,0:T(8,128)S(1)}, f32[12,193,64]{1,2,0:T(8,128)S(1)}, u32[]{:S(2)}, u32[]{:S(2)}) %collective-permute-start) | collective-permute-done | bytes 592928 | tf_op jit(solution)/shard_map/while/body/eval_jaxpr/ppermute | solution.py:11
  422.8 73.6 %all-gather.6.cloned.1.call-done = bf16[64,12,1024]{2,1,0:T(8,128)(2,1)} async-done(((bf16[1,12,1024]{2,1,0:T(8,128)(2,1)}), bf16[64,12,1024]{2,1,0:T(8,128)(2,1)}) %all-gather.6.cloned.1.call-update) | async-done | bytes 1572880 | tf_op jit(solution)/shard_map/while/body/eval_jaxpr/all_gather | solution.py:95
  507.7 17.6 %all-to-all-done = f32[64,12,128]{2,1,0:T(8,128)S(1)} async-done(((f32[64,12,128]{2,1,0:T(8,128)}), f32[64,12,128]{2,1,0:T(8,128)S(1)}, u32[]{:S(2)}, u32[]{:S(2)}) %all-to-all-start) | async-done | bytes 393248 | tf_op jit(solution)/shard_map/while/body/eval_jaxpr/all_to_all | solution.py:100
  534.7 17.0 %collective-permute-done = f32[12,193,64]{1,2,0:T(8,128)S(1)} collective-permute-done((f32[12,193,64]{1,2,0:T(8,128)S(1)}, f32[12,193,64]{1,2,0:T(8,128)S(1)}, u32[]{:S(2)}, u32[]{:S(2)}) %collective-permute-start) | collective-permute-done | bytes 592928 | tf_op jit(solution)/shard_map/while/body/eval_jaxpr/ppermute | solution.py:11
  553.1 19.5 %reduce-scatter.4.cloned.1.call-done = bf16[12,2048]{1,0:T(8,128)(2,1)} async-done(((bf16[12,8192]{1,0:T(8,128)(2,1)}), bf16[12,2048]{1,0:T(8,128)(2,1)}) %reduce-scatter.4.cloned.1.call-update) | async-done | bytes 49168 | tf_op jit(solution)/shard_map/reduce_scatter | solution.py:118
  574.1 643.4 %while.38 = (s32[]{:T(128)}, bf16[12,193,64]{1,2,0:T(8,128)(2,1)S(1)}, bf16[1,12,1024]{2,1,0:T(8,128)(2,1)}, bf16[12,8192]{1,0:T(8,128)(2,1)}, s32[]{:T(128)}, /...) while((s32[]{:T(128)}, ...), condition=%wide.region_6.7_spmd.clone, body=%wide.region_4.6_spmd.clone.sunk | while | flops 284812928 | bytes 31163484 | solution.py:173
  578.3 23.2 %all_to_all.76 = bf16[12,64,128]{2,0,1:T(8,128)(2,1)S(1)} all-to-all(bf16[12,64,128]{2,0,1:T(8,128)(2,1)S(1)} %copy.79), channel_id=1, replica_groups=mesh['grp'=4,'blk'=64] {'blk'}, dimensions={1} | all-to-all | bytes 393216 | tf_op jit(solution)/shard_map/while/body/eval_jaxpr/all_to_all | solution.py:149
  603.1 66.0 %fusion.73 = f32[16,1024]{1,0:T(8,128)S(1)} fusion(f32[768,1024]{1,0:T(8,128)S(1)} %fusion.72), kind=kCustom, calls=%all-reduce-scatter.clone.1 | all-reduce-scatter fusion | flops 1048577 | bytes 3212288 | tf_op jit(solution)/shard_map/while
  726.9 11.0 collective-permute-done.17
  742.1 18.3 %all_to_all.76 = bf16[12,64,128]{2,0,1:T(8,128)(2,1)S(1)} all-to-all(bf16[12,64,128]{2,0,1:T(8,128)(2,1)S(1)} %copy.79), channel_id=1, replica_groups=mesh['grp'=4,'blk'=64] {'blk'}, dimensions={1} | all-to-all | bytes 393216 | tf_op jit(solution)/shard_map/while/body/eval_jaxpr/all_to_all | solution.py:149
  762.0 67.0 %fusion.73 = f32[16,1024]{1,0:T(8,128)S(1)} fusion(f32[768,1024]{1,0:T(8,128)S(1)} %fusion.72), kind=kCustom, calls=%all-reduce-scatter.clone.1 | all-reduce-scatter fusion | flops 1048577 | bytes 3212288 | tf_op jit(solution)/shard_map/while
  902.0 18.3 %all_to_all.76 = bf16[12,64,128]{2,0,1:T(8,128)(2,1)S(1)} all-to-all(bf16[12,64,128]{2,0,1:T(8,128)(2,1)S(1)} %copy.79), channel_id=1, replica_groups=mesh['grp'=4,'blk'=64] {'blk'}, dimensions={1} | all-to-all | bytes 393216 | tf_op jit(solution)/shard_map/while/body/eval_jaxpr/all_to_all | solution.py:149
  921.8 67.0 %fusion.73 = f32[16,1024]{1,0:T(8,128)S(1)} fusion(f32[768,1024]{1,0:T(8,128)S(1)} %fusion.72), kind=kCustom, calls=%all-reduce-scatter.clone.1 | all-reduce-scatter fusion | flops 1048577 | bytes 3212288 | tf_op jit(solution)/shard_map/while
  1061.8 18.3 %all_to_all.76 = bf16[12,64,128]{2,0,1:T(8,128)(2,1)S(1)} all-to-all(bf16[12,64,128]{2,0,1:T(8,128)(2,1)S(1)} %copy.79), channel_id=1, replica_groups=mesh['grp'=4,'blk'=64] {'blk'}, dimensions={1} | all-to-all | bytes 393216 | tf_op jit(solution)/shard_map/while/body/eval_jaxpr/all_to_all | solution.py:149
  1081.7 67.0 %fusion.73 = f32[16,1024]{1,0:T(8,128)S(1)} fusion(f32[768,1024]{1,0:T(8,128)S(1)} %fusion.72), kind=kCustom, calls=%all-reduce-scatter.clone.1 | all-reduce-scatter fusion | flops 1048577 | bytes 3212288 | tf_op jit(solution)/shard_map/while
  (453 shorter events, 388.8 us)
Async XLA Ops:
  8.1 85.6 %all-gather.6.cloned.1.call-start = ((), (), s32[]{:S(2)}) async-start(), calls=%async_computation.4 | async-start | bytes 2129920 | tf_op jit(solution)/shard_map/while/body/eval_jaxpr/all_gather | solution.py:95
  98.1 24.6 %all-to-all-start = ((f32[64,12,128]{2,1,0:T(8,128)}), f32[64,12,128]{2,1,0:T(8,128)S(1)}, u32[]{:S(2)}, u32[]{:S(2)}) async-start(f32[64,12,128]{2,1,0:T(8,128)} %copy.72), calls=%async_computation | async-start | bytes 1048576 | tf_op jit(solution)/shard_map/while/body/eval_jaxpr/all_to_all | solution.py:100
  129.3 19.6 %collective-permute-start = (f32[12,193,64]{1,2,0:T(8,128)S(1)}, f32[12,193,64]{1,2,0:T(8,128)S(1)}, u32[]{:S(2)}, u32[]{:S(2)}) collective-permute-start(f32[12,193,64]{1,2,0:T(8,128)S(1)} %copy.75), channel_id=1, source_target_pairs={{0,64},{64,128},{128,192},{192,0},{1,65},{65,129},{129,193},{193,1... | collective-permute-start | bytes 1778696 | tf_op jit(solution)/shard_map/while/body/eval_jaxpr/ppermute | solution.py:11
  148.9 79.0 %all-gather.6.cloned.1.call-start = ((), (), s32[]{:S(2)}) async-start(), calls=%async_computation.4 | async-start | bytes 2129920 | tf_op jit(solution)/shard_map/while/body/eval_jaxpr/all_gather | solution.py:95
  232.3 24.6 %all-to-all-start = ((f32[64,12,128]{2,1,0:T(8,128)}), f32[64,12,128]{2,1,0:T(8,128)S(1)}, u32[]{:S(2)}, u32[]{:S(2)}) async-start(f32[64,12,128]{2,1,0:T(8,128)} %copy.72), calls=%async_computation | async-start | bytes 1048576 | tf_op jit(solution)/shard_map/while/body/eval_jaxpr/all_to_all | solution.py:100
  263.5 19.6 %collective-permute-start = (f32[12,193,64]{1,2,0:T(8,128)S(1)}, f32[12,193,64]{1,2,0:T(8,128)S(1)}, u32[]{:S(2)}, u32[]{:S(2)}) collective-permute-start(f32[12,193,64]{1,2,0:T(8,128)S(1)} %copy.75), channel_id=1, source_target_pairs={{0,64},{64,128},{128,192},{192,0},{1,65},{65,129},{129,193},{193,1... | collective-permute-start | bytes 1778696 | tf_op jit(solution)/shard_map/while/body/eval_jaxpr/ppermute | solution.py:11
  283.2 79.0 %all-gather.6.cloned.1.call-start = ((), (), s32[]{:S(2)}) async-start(), calls=%async_computation.4 | async-start | bytes 2129920 | tf_op jit(solution)/shard_map/while/body/eval_jaxpr/all_gather | solution.py:95
  366.6 24.6 %all-to-all-start = ((f32[64,12,128]{2,1,0:T(8,128)}), f32[64,12,128]{2,1,0:T(8,128)S(1)}, u32[]{:S(2)}, u32[]{:S(2)}) async-start(f32[64,12,128]{2,1,0:T(8,128)} %copy.72), calls=%async_computation | async-start | bytes 1048576 | tf_op jit(solution)/shard_map/while/body/eval_jaxpr/all_to_all | solution.py:100
  397.8 19.6 %collective-permute-start = (f32[12,193,64]{1,2,0:T(8,128)S(1)}, f32[12,193,64]{1,2,0:T(8,128)S(1)}, u32[]{:S(2)}, u32[]{:S(2)}) collective-permute-start(f32[12,193,64]{1,2,0:T(8,128)S(1)} %copy.75), channel_id=1, source_target_pairs={{0,64},{64,128},{128,192},{192,0},{1,65},{65,129},{129,193},{193,1... | collective-permute-start | bytes 1778696 | tf_op jit(solution)/shard_map/while/body/eval_jaxpr/ppermute | solution.py:11
  417.4 79.0 %all-gather.6.cloned.1.call-start = ((), (), s32[]{:S(2)}) async-start(), calls=%async_computation.4 | async-start | bytes 2129920 | tf_op jit(solution)/shard_map/while/body/eval_jaxpr/all_gather | solution.py:95
  500.8 24.6 %all-to-all-start = ((f32[64,12,128]{2,1,0:T(8,128)}), f32[64,12,128]{2,1,0:T(8,128)S(1)}, u32[]{:S(2)}, u32[]{:S(2)}) async-start(f32[64,12,128]{2,1,0:T(8,128)} %copy.72), calls=%async_computation | async-start | bytes 1048576 | tf_op jit(solution)/shard_map/while/body/eval_jaxpr/all_to_all | solution.py:100
  532.0 19.6 %collective-permute-start = (f32[12,193,64]{1,2,0:T(8,128)S(1)}, f32[12,193,64]{1,2,0:T(8,128)S(1)}, u32[]{:S(2)}, u32[]{:S(2)}) collective-permute-start(f32[12,193,64]{1,2,0:T(8,128)S(1)} %copy.75), channel_id=1, source_target_pairs={{0,64},{64,128},{128,192},{192,0},{1,65},{65,129},{129,193},{193,1... | collective-permute-start | bytes 1778696 | tf_op jit(solution)/shard_map/while/body/eval_jaxpr/ppermute | solution.py:11
  551.7 21.0 %reduce-scatter.4.cloned.1.call-start = ((), (), s32[]{:S(2)}) async-start(), calls=%async_computation.3 | async-start | bytes 327680 | tf_op jit(solution)/shard_map/reduce_scatter | solution.py:118
  669.1 17.6 %collective-permute-start.1 = (f32[12,1024]{1,0:T(8,128)S(1)}, f32[12,1024]{1,0:T(8,128)S(1)}, u32[]{:S(2)}, u32[]{:S(2)}) collective-permute-start(f32[12,1024]{1,0:T(8,128)S(1)} %slice.162), channel_id=1, source_target_pairs={{0,16},{1,17},{2,18},{3,19},{4,20},{5,21},{6,22},{7,23},{8,24},{9,... | collective-permute-start | bytes 147464 | tf_op jit(solution)/shard_map/while
  671.9 16.1 %collective-permute-start.2 = (f32[16,1024]{1,0:T(8,128)S(1)}, f32[16,1024]{1,0:T(8,128)S(1)}, u32[]{:S(2)}, u32[]{:S(2)}) collective-permute-start(f32[16,1024]{1,0:T(8,128)S(1)} %fusion.73), channel_id=1, source_target_pairs={{0,15},{1,16},{2,17},{3,18},{4,19},{5,20},{6,21},{7,22},{8,23},{9,... | collective-permute-start | bytes 196616 | tf_op jit(solution)/shard_map/while
  674.5 17.2 %collective-permute-start.3 = (f32[16,1024]{1,0:T(8,128)S(1)}, f32[16,1024]{1,0:T(8,128)S(1)}, u32[]{:S(2)}, u32[]{:S(2)}) collective-permute-start(f32[16,1024]{1,0:T(8,128)S(1)} %fusion.73), channel_id=1, source_target_pairs={{0,14},{1,15},{2,16},{3,17},{4,18},{5,19},{6,20},{7,21},{8,22},{9,... | collective-permute-start | bytes 196616 | tf_op jit(solution)/shard_map/while
  829.0 17.6 %collective-permute-start.1 = (f32[12,1024]{1,0:T(8,128)S(1)}, f32[12,1024]{1,0:T(8,128)S(1)}, u32[]{:S(2)}, u32[]{:S(2)}) collective-permute-start(f32[12,1024]{1,0:T(8,128)S(1)} %slice.162), channel_id=1, source_target_pairs={{0,16},{1,17},{2,18},{3,19},{4,20},{5,21},{6,22},{7,23},{8,24},{9,... | collective-permute-start | bytes 147464 | tf_op jit(solution)/shard_map/while
  831.8 16.1 %collective-permute-start.2 = (f32[16,1024]{1,0:T(8,128)S(1)}, f32[16,1024]{1,0:T(8,128)S(1)}, u32[]{:S(2)}, u32[]{:S(2)}) collective-permute-start(f32[16,1024]{1,0:T(8,128)S(1)} %fusion.73), channel_id=1, source_target_pairs={{0,15},{1,16},{2,17},{3,18},{4,19},{5,20},{6,21},{7,22},{8,23},{9,... | collective-permute-start | bytes 196616 | tf_op jit(solution)/shard_map/while
  834.3 17.2 %collective-permute-start.3 = (f32[16,1024]{1,0:T(8,128)S(1)}, f32[16,1024]{1,0:T(8,128)S(1)}, u32[]{:S(2)}, u32[]{:S(2)}) collective-permute-start(f32[16,1024]{1,0:T(8,128)S(1)} %fusion.73), channel_id=1, source_target_pairs={{0,14},{1,15},{2,16},{3,17},{4,18},{5,19},{6,20},{7,21},{8,22},{9,... | collective-permute-start | bytes 196616 | tf_op jit(solution)/shard_map/while
  988.9 17.6 %collective-permute-start.1 = (f32[12,1024]{1,0:T(8,128)S(1)}, f32[12,1024]{1,0:T(8,128)S(1)}, u32[]{:S(2)}, u32[]{:S(2)}) collective-permute-start(f32[12,1024]{1,0:T(8,128)S(1)} %slice.162), channel_id=1, source_target_pairs={{0,16},{1,17},{2,18},{3,19},{4,20},{5,21},{6,22},{7,23},{8,24},{9,... | collective-permute-start | bytes 147464 | tf_op jit(solution)/shard_map/while
  991.7 16.1 %collective-permute-start.2 = (f32[16,1024]{1,0:T(8,128)S(1)}, f32[16,1024]{1,0:T(8,128)S(1)}, u32[]{:S(2)}, u32[]{:S(2)}) collective-permute-start(f32[16,1024]{1,0:T(8,128)S(1)} %fusion.73), channel_id=1, source_target_pairs={{0,15},{1,16},{2,17},{3,18},{4,19},{5,20},{6,21},{7,22},{8,23},{9,... | collective-permute-start | bytes 196616 | tf_op jit(solution)/shard_map/while
  994.2 17.2 %collective-permute-start.3 = (f32[16,1024]{1,0:T(8,128)S(1)}, f32[16,1024]{1,0:T(8,128)S(1)}, u32[]{:S(2)}, u32[]{:S(2)}) collective-permute-start(f32[16,1024]{1,0:T(8,128)S(1)} %fusion.73), channel_id=1, source_target_pairs={{0,14},{1,15},{2,16},{3,17},{4,18},{5,19},{6,20},{7,21},{8,22},{9,... | collective-permute-start | bytes 196616 | tf_op jit(solution)/shard_map/while
  1148.7 17.6 %collective-permute-start.1 = (f32[12,1024]{1,0:T(8,128)S(1)}, f32[12,1024]{1,0:T(8,128)S(1)}, u32[]{:S(2)}, u32[]{:S(2)}) collective-permute-start(f32[12,1024]{1,0:T(8,128)S(1)} %slice.162), channel_id=1, source_target_pairs={{0,16},{1,17},{2,18},{3,19},{4,20},{5,21},{6,22},{7,23},{8,24},{9,... | collective-permute-start | bytes 147464 | tf_op jit(solution)/shard_map/while
  1154.1 17.2 %collective-permute-start.3 = (f32[16,1024]{1,0:T(8,128)S(1)}, f32[16,1024]{1,0:T(8,128)S(1)}, u32[]{:S(2)}, u32[]{:S(2)}) collective-permute-start(f32[16,1024]{1,0:T(8,128)S(1)} %fusion.73), channel_id=1, source_target_pairs={{0,14},{1,15},{2,16},{3,17},{4,18},{5,19},{6,20},{7,21},{8,22},{9,... | collective-permute-start | bytes 196616 | tf_op jit(solution)/shard_map/while
  (107 other events, 1690.4 us)
Sparse Core Ops, SparseCore 0:
  13.7 79.9 all-gather.5
  154.4 73.4 all-gather.5
  288.7 73.4 all-gather.5
  422.9 73.4 all-gather.5
Sparse Core Ops, SparseCore 1:
  554.6 17.9 reduce-scatter.3
where the time goes:
time: 1230 us; the launch traced here: 1220 us
  waiting for transfers between devices  504 us (41%)
  blocking collectives  345 us (28%)
  starting transfers between devices  219 us (18%)
  local copies, waits for them, and re-layouts  64.5 us (5%)
  matrix products  36.2 us (3%)
  other arithmetic  35.8 us (3%)
  between operations  15.2 us (1%)
    all_gather x4, waiting for transfers between devices, forward_step(): lax.all_gather(solved, 'blk', axis=0, tiled=True)  301 us
    while x4, blocking collectives  267 us
    while x64, starting transfers between devices  184 us
    ppermute x8, waiting for transfers between devices, shifted(): return lax.ppermute(x, axis, [(i, (i + by) % count) for i in range(count)])  113 us
    all_to_all x4, blocking collectives, backward_step(): lax.all_to_all(selected_rows, 'blk', split_axis=1, concat_axis=0, tiled=T...  78.1 us
    all_to_all x4, waiting for transfers between devices, forward_step(): lax.all_to_all(products, 'blk', split_axis=0, concat_axis=1, tiled=True)  70.5 us
    while x116, local copies, waits for them, and re-layouts  37.9 us
    all_to_all x4, starting transfers between devices, forward_step(): lax.all_to_all(products, 'blk', split_axis=0, concat_axis=1, tiled=True)  27.6 us
  transfers between devices with their start and end apart: 81, of which 17 were waited for; matrix products, arithmetic and copies ran while one was open for 1% of the time, Pallas kernels for 0%

commit v1 on v0

v1 whole, which is shorter than its diff:
```python
import functools

import jax
import jax.numpy as jnp
from jax import lax
from jax.experimental import pallas as pl
from jax.experimental.pallas import tpu as pltpu
from jax.sharding import PartitionSpec as P

TILE = 64
ROWS = 16
CHUNK = 16
GROUPS = 4
BF = jnp.bfloat16
F32 = jnp.float32
VMEM_LIMIT = 48 * 1024 * 1024
NT = (((1,), (1,)), ((), ()))


def mm(a, b):
    return jnp.dot(a, b, preferred_element_type=F32)


def mm_nt(a, b):
    return lax.dot_general(a, b, NT, preferred_element_type=F32)


def split_mm(product, r, w):
    high = r.astype(BF)
    low = (r - high.astype(F32)).astype(BF)
    both = product(jnp.concatenate([high, low], axis=0), w)
    return both[: r.shape[0]] + both[r.shape[0] :]


def lower_solve(residue, inverse, coupling):
    half = coupling.shape[0]
    leading = split_mm(mm, residue[:, :half], inverse[:half]).astype(BF)
    carried = residue[:, half:] - mm(leading, coupling[...])
    second = split_mm(mm, carried, inverse[half:]).astype(BF)
    return leading, second


def upper_solve(residue, inverse, coupling):
    half = coupling.shape[0]
    second = split_mm(mm_nt, residue[:, half:], inverse[half:]).astype(BF)
    carried = residue[:, :half] - mm_nt(second, coupling[...])
    leading = split_mm(mm_nt, carried, inverse[:half]).astype(BF)
    return leading, second


def fetch_tiles(slots, factor, tiles, sems):
    copies = []
    for i in range(CHUNK):
        start = pl.multiple_of(slots[i] * TILE, TILE)
        copy = pltpu.make_async_copy(
            factor.at[pl.ds(start, TILE)], tiles.at[pl.ds(i * TILE, TILE)], sems.at[i]
        )
        copy.start()
        copies.append(copy)
    return copies


def forward_kernel(received_count, slots, factor, mask, acc, inverse, coupling, *rest):
    received = rest[:received_count]
    acc_out, solved_out, message_out, tiles, sems = rest[received_count:]
    copies = fetch_tiles(slots, factor, tiles, sems)
    residue = acc[...]
    for ref in received:
        residue = residue - ref[...].astype(F32)
    acc_out[...] = residue
    half = coupling.shape[0]
    leading, second = lower_solve(residue, inverse, coupling)
    solved_out[:, :half] = leading
    solved_out[:, half:] = second
    for copy in copies:
        copy.wait()
    product = mm_nt(solved_out[...], tiles[...])
    message_out[...] = (product * mask[...]).astype(BF)


def backward_kernel(received_count, slots, factor, mask, acc, inverse, coupling, *rest):
    received = rest[:received_count]
    acc_out, solved_out = rest[received_count : received_count + 2]
    residue = acc[...]
    if received:
        tiles, sems = rest[received_count + 2 :]
        copies = fetch_tiles(slots, factor, tiles, sems)
        for ref in received[1:]:
            residue = residue - ref[...]
        masked = received[0][...] * mask[...].astype(BF)
        for copy in copies:
            copy.wait()
        residue = residue - mm(masked, tiles[...])
    acc_out[...] = residue
    half = coupling.shape[0]
    leading, second = upper_solve(residue, inverse, coupling)
    solved_out[:, :half] = leading
    solved_out[:, half:] = second


def whole(x):
    return pl.BlockSpec(x.shape, lambda i, *_: (0,) * len(x.shape))


def chain_call(kernel, slots, factor, mask, acc, inverse, coupling, received, out_shapes, with_tiles):
    width = acc.shape[1]
    operands = [mask, acc, inverse, coupling, *received]
    scratch = []
    if with_tiles:
        scratch = [
            pltpu.VMEM((CHUNK * TILE, width), BF),
            pltpu.SemaphoreType.DMA((CHUNK,)),
        ]
    return pl.pallas_call(
        functools.partial(kernel, len(received)),
        grid_spec=pltpu.PrefetchScalarGridSpec(
            num_scalar_prefetch=1,
            grid=(1,),
            in_specs=[pl.BlockSpec(memory_space=pl.ANY)] + [whole(x) for x in operands],
            out_specs=[whole(x) for x in out_shapes],
            scratch_shapes=scratch,
        ),
        out_shape=out_shapes,
        compiler_params=pltpu.CompilerParams(vmem_limit_bytes=VMEM_LIMIT),
        cost_estimate=pl.CostEstimate(
            flops=4 * ROWS * width * width, bytes_accessed=8 * width * width, transcendentals=0
        ),
    )(slots, factor, *operands)


def tile_specs(width):
    def spec(j):
        return pl.BlockSpec((TILE, width), lambda i, slots: (slots[i * CHUNK + j], 0))

    return [spec(j) for j in range(CHUNK)]


def spread_kernel(slots, solved, mask, *rest):
    tiles, out = rest[:CHUNK], rest[CHUNK]
    stacked = jnp.concatenate([t[...] for t in tiles], axis=0)
    out[...] = (mm_nt(solved[...], stacked) * mask[...]).astype(out.dtype)


def spread(slots, solved, mask, factor):
    width = solved.shape[1]
    count = slots.shape[0] // CHUNK
    return pl.pallas_call(
        spread_kernel,
        grid_spec=pltpu.PrefetchScalarGridSpec(
            num_scalar_prefetch=1,
            grid=(count,),
            in_specs=[
                pl.BlockSpec((ROWS, width), lambda i, slots: (0, 0)),
                pl.BlockSpec((1, CHUNK * TILE), lambda i, slots: (0, i)),
            ]
            + tile_specs(width),
            out_specs=pl.BlockSpec((ROWS, CHUNK * TILE), lambda i, slots: (0, i)),
        ),
        out_shape=jax.ShapeDtypeStruct((ROWS, count * CHUNK * TILE), BF),
        compiler_params=pltpu.CompilerParams(vmem_limit_bytes=VMEM_LIMIT),
        cost_estimate=pl.CostEstimate(
            flops=2 * ROWS * width * width * count,
            bytes_accessed=2 * width * width * count,
            transcendentals=0,
        ),
    )(slots, solved, mask, *([factor] * CHUNK))


def collect_kernel(slots, rows, mask, *rest):
    tiles, out = rest[:CHUNK], rest[CHUNK]

    @pl.when(pl.program_id(0) == 0)
    def _():
        out[...] = jnp.zeros_like(out)

    stacked = jnp.concatenate([t[...] for t in tiles], axis=0)
    out[...] += mm(rows[...] * mask[...].astype(BF), stacked)


def collect(slots, rows, mask, factor):
    width = factor.shape[1]
    count = slots.shape[0] // CHUNK
    return pl.pallas_call(
        collect_kernel,
        grid_spec=pltpu.PrefetchScalarGridSpec(
            num_scalar_prefetch=1,
            grid=(count,),
            in_specs=[
                pl.BlockSpec((ROWS, CHUNK * TILE), lambda i, slots: (0, i)),
                pl.BlockSpec((1, CHUNK * TILE), lambda i, slots: (0, i)),
            ]
            + tile_specs(width),
            out_specs=pl.BlockSpec((ROWS, width), lambda i, slots: (0, 0)),
        ),
        out_shape=jax.ShapeDtypeStruct((ROWS, width), F32),
        compiler_params=pltpu.CompilerParams(vmem_limit_bytes=VMEM_LIMIT),
        cost_estimate=pl.CostEstimate(
            flops=2 * ROWS * width * width * count,
            bytes_accessed=2 * width * width * count,
            transcendentals=0,
        ),
    )(slots, rows, mask, *([factor] * CHUNK))


def body(rhs, lower_factor_tiles, tile_rows, diag_inv, inner_block, lower_row_solution):
    _, cases, width = rhs.shape
    group = lax.axis_index("grp")
    table = tile_rows[0, 0]
    slot_count = table.shape[0]
    inverse, coupling = diag_inv[0], inner_block[0]
    per_panel = width // TILE
    chain_tiles = GROUPS * per_panel
    lower_tiles = lower_row_solution.shape[1] // TILE
    tile_count = chain_tiles + lower_tiles

    def grow(x):
        return jnp.pad(x, ((0, ROWS - cases), (0, 0)))

    def send(x, pairs):
        return lax.ppermute(x, "grp", pairs)

    here = table[None, :] == jnp.arange(tile_count, dtype=jnp.int32)[:, None]
    slot_of = jnp.sum(
        jnp.where(here, jnp.arange(slot_count, dtype=jnp.int32)[None, :], 0), axis=1
    )
    present = jnp.any(here, axis=1)
    numbers = jnp.arange(tile_count, dtype=jnp.int32)
    first = (group + 1) * per_panel
    near_slots = lax.dynamic_slice_in_dim(slot_of, first, 3 * per_panel)
    near_mask = lax.dynamic_slice_in_dim(present & (numbers < chain_tiles), first, 3 * per_panel)
    quarter = lower_tiles // GROUPS
    turned = lambda x: jnp.roll(x.reshape(GROUPS, quarter), -group, axis=0).reshape(-1)
    wide = lambda m: jnp.repeat(m.astype(F32), TILE)[None, :]
    low_slots, low_present = slot_of[chain_tiles:], present[chain_tiles:]
    low_mask = wide(low_present)
    turned_slots, turned_mask = turned(low_slots), wide(turned(low_present))
    near_mask = wide(near_mask)
    panel = per_panel * TILE
    slots1, mask1 = near_slots[:per_panel], near_mask[:, :panel]
    slots23, mask23 = near_slots[per_panel:], near_mask[:, panel:]

    factor = lax.all_gather(lower_factor_tiles[0], "blk", axis=0, tiled=True)

    rows_shape = lambda dtype: jax.ShapeDtypeStruct((ROWS, width), dtype)
    owed_low = collect(low_slots, grow(lower_row_solution), low_mask, factor)

    acc = grow(rhs[0]).astype(F32)
    received, later = [], {}
    for step in range(GROUPS):
        acc, solved, message = chain_call(
            forward_kernel, slots1, factor, mask1, acc, inverse, coupling, received,
            [rows_shape(F32), rows_shape(BF), rows_shape(BF)], True,
        )
        if step == GROUPS - 1:
            break
        received = [send(message, [(step, step + 1)])]
        if step + 2 < GROUPS:
            far = spread(slots23, solved, mask23, factor)
            for hop in range(2, GROUPS - step):
                part = far[:, (hop - 2) * panel : (hop - 1) * panel]
                later.setdefault(step + 2, []).append(send(part, [(step, step + hop)]))
        received += later.pop(step + 1, [])

    beyond = spread(turned_slots, solved, turned_mask, factor)[:cases]
    part = lower_tiles * TILE // GROUPS
    pending = beyond[:, :part].astype(F32)
    for hop in range(1, GROUPS):
        pending = pending + send(
            beyond[:, hop * part : (hop + 1) * part],
            [(g, (g + hop) % GROUPS) for g in range(GROUPS)],
        ).astype(F32)

    acc = solved.astype(F32) - owed_low
    received = []
    for step in range(GROUPS):
        acc, settled = chain_call(
            backward_kernel, slots1, factor, mask1, acc, inverse, coupling, received,
            [rows_shape(F32), rows_shape(BF)], bool(received),
        )
        if step == GROUPS - 1:
            break
        holder = GROUPS - 1 - step
        received = [send(settled, [(holder, holder - 1)])]
        if holder >= 2:
            far = [send(settled, [(holder, holder - hop)]) for hop in range(2, holder + 1)]
            while len(far) < 2:
                far.append(jnp.zeros_like(settled))
            later.setdefault(step + 2, []).append(
                collect(slots23, jnp.concatenate(far, axis=1), mask23, factor)
            )
        received += later.pop(step + 1, [])

    return (solved[None, :cases], pending, settled[None, :cases])


def solution(mesh):
    placed = (
        P(None, "blk", "grp"),
        P(None, ("grp", "blk"), None),
        P(None, "grp", None),
        P(None, "grp", None),
        P(None, "grp", None),
        P("blk", None),
    )
    return jax.shard_map(
        body,
        mesh=mesh,
        in_specs=placed,
        out_specs=(P(None, "blk", "grp"), P("blk", "grp"), P(None, "blk", "grp")),
        check_vma=False,
    )
```

time: 1230 us -> 211 us (0.17)
  waiting for transfers between devices: 504 us -> 102 us
  blocking collectives: 345 us -> 0 us
  starting transfers between devices: 219 us -> 23.3 us
  Pallas kernels: 0 us -> 60.8 us
  local copies, waits for them, and re-layouts: 64.5 us -> 4.7 us
  matrix products: 36.2 us -> 0 us
  other arithmetic: 35.8 us -> 4.3 us
    while x4 -> x0, blocking collectives: 267 us -> none
    all_gather x4 -> x1, waiting for transfers between devices: 301 us -> 101 us  [body(): factor = lax.all_gather(lower_factor_tiles[0], 'blk', axis=0, tiled=True)]
    while x64 -> x0, starting transfers between devices: 184 us -> none
    ppermute x8 -> x15, waiting for transfers between devices: 113 us -> 0.04 us  [send(): return lax.ppermute(x, 'grp', pairs)]
    all_to_all x4 -> x0, blocking collectives: 78.1 us -> none  [backward_step(): lax.all_to_all(selected_rows, 'blk', split_axis=1, concat_axis=0, tiled=T...]
    all_to_all x4 -> x0, waiting for transfers between devices: 70.5 us -> none  [forward_step(): lax.all_to_all(products, 'blk', split_axis=0, concat_axis=1, tiled=True)]
    pallas_call x0 -> x14, Pallas kernels: none -> 60.8 us  [the longest x8 24.3 us: chain_call(): pl.pallas_call(functools.partial(kernel, len(received)), grid_spec=pltpu....]
    while x116 -> x0, local copies, waits for them, and re-layouts: 37.9 us -> none
  transfers between devices with their start and end apart: 81 -> 16, of which waited for: 17 -> 1; matrix products, arithmetic and copies ran while one was open for 1% -> 3% of each run, Pallas kernels for 0% -> 24%
where the time goes in v1:
time: 211 us; the launch traced here: 210 us
  waiting for transfers between devices  102 us (48%)
  Pallas kernels  60.8 us (29%)
  starting transfers between devices  23.3 us (11%)
  between operations  14.6 us (7%)
  local copies, waits for them, and re-layouts  4.7 us (2%)
  other arithmetic  4.3 us (2%)
    all_gather x1, waiting for transfers between devices, body(): factor = lax.all_gather(lower_factor_tiles[0], 'blk', axis=0, tiled=True)  101 us
    pallas_call x8, Pallas kernels, chain_call(): pl.pallas_call(functools.partial(kernel, len(received)), grid_spec=pltpu....  24.3 us
    ppermute x15, starting transfers between devices, send(): return lax.ppermute(x, 'grp', pairs)  23.3 us
    pallas_call x3, Pallas kernels, spread(): pl.pallas_call(spread_kernel, grid_spec=pltpu.PrefetchScalarGridSpec(num_...  19.3 us
    pallas_call x3, Pallas kernels, collect(): pl.pallas_call(collect_kernel, grid_spec=pltpu.PrefetchScalarGridSpec(num...  17.2 us
  transfers between devices with their start and end apart: 16, of which 1 were waited for; matrix products, arithmetic and copies ran while one was open for 3% of the time, Pallas kernels for 24%

profile of v1, /device:TPU:16, one launch (start us, length us, event | category | flops | bytes accessed | tf_op | source)
XLA Modules:
  0.0 209.6 jit_solution(9830187781595907239)
XLA Ops:
  12.1 101.2 %all-gather.3.cloned.1.call-done = bf16[1,8192,1024]{2,1,0:T(8,128)(2,1)} async-done(((bf16[1,128,1024]{2,1,0:T(8,128)(2,1)}), bf16[1,8192,1024]{2,1,0:T(8,128)(2,1)}) %all-gather.3.cloned.1.call-update) | async-done | bytes 16777232 | tf_op jit(solution)/shard_map/all_gather | solution.py:242
  113.3 1.2 copy-done
  115.5 3.1 %shard_map.85 = (f32[16,1024]{1,0:T(8,128)S(1)}, bf16[16,1024]{1,0:T(8,128)(2,1)S(1)}, bf16[16,1024]{1,0:T(8,128)(2,1)S(1)}) custom-call(s32[16]{0:T(128)S(1)} %bitcast.26, bf16[8192,1024]{1,0:T(8,128)(2,1)} %bitcast.34, f32[1,1024]{1,0:T(1,128)S(1)} %slice.81.mask, f32[16,1024]{1,0:T(8,128)S(1)} %pad_convert_fusion.acc, bf16[1024,512]{1,0:T(8,128)(2,1)S(1)} %bitcast.10, ...), custom_call_target="tpu_custom_call" | custom-call | flops 67108864 | bytes 8388608 | tf_op jit(solution)/shard_map/pallas_call | solution.py:114
  119.4 3.9 %shard_map.87 = bf16[16,2048]{1,0:T(8,128)(2,1)S(1)} custom-call(s32[32]{0:T(128)S(1)} %slice.68.slots, bf16[16,1024]{1,0:T(8,128)(2,1)S(1)} %get-tuple-element.23.solved, f32[1,2048]{1,0:T(1,128)S(1)} %slice.82.mask, bf16[8192,1024]{1,0:T(8,128)(2,1)} %bitcast.35, bf16[8192,1024]{1,0:T(8,128)(2,1)} %bitcast.36, bf16[8192,1024]{1,0:T(8,128)(2,1)} %bitcast.37, ...), custom_call_target="tpu_custom_call" | custom-call | flops 67108864 | bytes 4194304 | tf_op jit(solution)/shard_map/pallas_call | solution.py:147
  123.4 1.3 collective-permute-start.2
  125.4 3.2 %shard_map.86 = (f32[16,1024]{1,0:T(8,128)S(1)}, bf16[16,1024]{1,0:T(8,128)(2,1)S(1)}, bf16[16,1024]{1,0:T(8,128)(2,1)S(1)}) custom-call(s32[16]{0:T(128)S(1)} %bitcast.27, bf16[8192,1024]{1,0:T(8,128)(2,1)} %bitcast.51, f32[1,1024]{1,0:T(1,128)S(1)} %slice.81.mask, f32[16,1024]{1,0:T(8,128)S(1)} %get-tuple-element.19.acc, bf16[1024,512]{1,0:T(8,128)(2,1)S(1)} %bitcast.11, ...), custom_call_target="tpu_custom_call" | custom-call | flops 67108864 | bytes 8388608 | tf_op jit(solution)/shard_map/pallas_call | solution.py:114
  128.6 1.3 collective-permute-start.1
  129.9 3.9 %shard_map.89 = bf16[16,2048]{1,0:T(8,128)(2,1)S(1)} custom-call(s32[32]{0:T(128)S(1)} %slice.68.slots, bf16[16,1024]{1,0:T(8,128)(2,1)S(1)} %get-tuple-element.26.solved, f32[1,2048]{1,0:T(1,128)S(1)} %slice.82.mask, bf16[8192,1024]{1,0:T(8,128)(2,1)} %bitcast.52, bf16[8192,1024]{1,0:T(8,128)(2,1)} %bitcast.53, bf16[8192,1024]{1,0:T(8,128)(2,1)} %bitcast.54, ...), custom_call_target="tpu_custom_call" | custom-call | flops 67108864 | bytes 4194304 | tf_op jit(solution)/shard_map/pallas_call | solution.py:147
  134.7 3.2 %shard_map.88 = (f32[16,1024]{1,0:T(8,128)S(1)}, bf16[16,1024]{1,0:T(8,128)(2,1)}, bf16[16,1024]{1,0:T(8,128)(2,1)S(1)}) custom-call(s32[16]{0:T(128)S(1)} %bitcast.28, bf16[8192,1024]{1,0:T(8,128)(2,1)} %bitcast.68, f32[1,1024]{1,0:T(1,128)S(1)} %slice.81.mask, f32[16,1024]{1,0:T(8,128)S(1)} %get-tuple-element.21.acc, bf16[1024,512]{1,0:T(8,128)(2,1)S(1)} %bitcast.12, ...), custom_call_target="tpu_custom_call" | custom-call | flops 67108864 | bytes 8388608 | tf_op jit(solution)/shard_map/pallas_call | solution.py:114
  137.9 2.9 %collective-permute-start.4 = (bf16[16,1024]{1,0:T(8,128)(2,1)S(1)}, bf16[16,1024]{1,0:T(8,128)(2,1)S(1)}, u32[]{:S(2)}, u32[]{:S(2)}) collective-permute-start(bf16[16,1024]{1,0:T(8,128)(2,1)S(1)} %get-tuple-element.25), channel_id=1, source_target_pairs={{128,192},{129,193},{130,194},{131,195},{132,196},{133,197},{134,1... | collective-permute-start | bytes 98312 | tf_op jit(solution)/shard_map/ppermute | solution.py:220
  141.4 10.2 %shard_map.92 = f32[16,1024]{1,0:T(8,128)S(1)} custom-call(s32[128]{0:T(128)S(1)} %copy-done.7, bf16[16,8192]{1,0:T(8,128)(2,1)S(1)} %pad.10.rows, f32[1,8192]{1,0:T(1,128)S(1)} %broadcast_in_dim_reshape.11.mask, bf16[8192,1024]{1,0:T(8,128)(2,1)} %bitcast.69, bf16[8192,1024]{1,0:T(8,128)(2,1)} %bitcast.70, bf16[8192,1024]{1,0:T(8,128)(2,1)} %bitcast.71, ...), custom_call_target="tpu_custom_call" | custom-call | flops 268435456 | bytes 16777216 | tf_op jit(solution)/shard_map/pallas_call | solution.py:183
  151.7 3.8 %shard_map.90 = (f32[16,1024]{1,0:T(8,128)}, bf16[16,1024]{1,0:T(8,128)(2,1)S(1)}, bf16[16,1024]{1,0:T(8,128)(2,1)}) custom-call(s32[16]{0:T(128)S(1)} %bitcast.29, bf16[8192,1024]{1,0:T(8,128)(2,1)} %bitcast.85, f32[1,1024]{1,0:T(1,128)S(1)} %slice.81.mask, f32[16,1024]{1,0:T(8,128)S(1)} %get-tuple-element.24.acc, bf16[1024,512]{1,0:T(8,128)(2,1)S(1)} %bitcast.13, ...), custom_call_target="tpu_custom_call" | custom-call | flops 67108864 | bytes 8388608 | tf_op jit(solution)/shard_map/pallas_call | solution.py:114
  155.6 1.2 shard_map.93
  158.1 1.3 collective-permute-start.9
  159.4 11.5 %shard_map.91 = bf16[16,8192]{1,0:T(8,128)(2,1)S(1)} custom-call(s32[128]{0:T(128)S(1)} %reshape.36.slots, bf16[16,1024]{1,0:T(8,128)(2,1)S(1)} %get-tuple-element.27.solved, f32[1,8192]{1,0:T(1,128)S(1)} %broadcast_in_dim_reshape.10.mask, bf16[8192,1024]{1,0:T(8,128)(2,1)} %bitcast.87, bf16[8192,1024]{1,0:T(8,128)(2,1)} %bitcast.88, ...), custom_call_target="tpu_custom_call" | custom-call | flops 268435456 | bytes 16777216 | tf_op jit(solution)/shard_map/pallas_call | solution.py:147
  171.5 5.0 %collective-permute-start.6 = (bf16[12,2048]{1,0:T(8,128)(2,1)S(1)}, bf16[12,2048]{1,0:T(8,128)(2,1)S(1)}, u32[]{:S(2)}, u32[]{:S(2)}) collective-permute-start(bf16[12,2048]{1,0:T(8,128)(2,1)S(1)} %get-tuple-element.35), channel_id=1, source_target_pairs={{0,64},{64,128},{128,192},{192,0},{1,65},{65,129},{129,193},{193,1... | collective-permute-start | bytes 147464 | tf_op jit(solution)/shard_map/ppermute | solution.py:220
  176.6 1.5 collective-permute-start.8
  178.0 3.3 %shard_map.94 = (f32[16,1024]{1,0:T(8,128)S(1)}, bf16[16,1024]{1,0:T(8,128)(2,1)S(1)}) custom-call(s32[16]{0:T(128)S(1)} %bitcast.31, bf16[8192,1024]{1,0:T(8,128)(2,1)} %bitcast.103, f32[1,1024]{1,0:T(1,128)S(1)} %slice.81.mask, f32[16,1024]{1,0:T(8,128)S(1)} %get-tuple-element.28.acc, bf16[1024,512]{1,0:T(8,128)(2,1)S(1)} %bitcast.15, ...), custom_call_target="tpu_custom_call" | custom-call | flops 67108864 | bytes 8388608 | tf_op jit(solution)/shard_map/pallas_call | solution.py:114
  181.3 4.5 %collective-permute-start.10 = (bf16[16,1024]{1,0:T(8,128)(2,1)S(1)}, bf16[16,1024]{1,0:T(8,128)(2,1)S(1)}, u32[]{:S(2)}, u32[]{:S(2)}) collective-permute-start(bf16[16,1024]{1,0:T(8,128)(2,1)S(1)} %get-tuple-element.31), channel_id=1, source_target_pairs={{128,64},{129,65},{130,66},{131,67},{132,68},{133,69},{134,70},{13... | collective-permute-start | bytes 98312 | tf_op jit(solution)/shard_map/ppermute | solution.py:220
  185.9 1.3 collective-permute-start.14
  187.2 3.5 %shard_map.95.rest_1_ = f32[16,1024]{1,0:T(8,128)S(1)} custom-call(s32[32]{0:T(128)S(1)} %copy-done.5, bf16[16,2048]{1,0:T(8,128)(2,1)S(1)} %pad_maximum_fusion.rows, f32[1,2048]{1,0:T(1,128)S(1)} %slice.82.mask, bf16[8192,1024]{1,0:T(8,128)(2,1)} %bitcast.104, bf16[8192,1024]{1,0:T(8,128)(2,1)} %bitcast.105, bf16[8192,1024]{1,0:T(8,128)(2,1)} %bitcast.106, ...), custom_call_target="tpu_custom_call" | custom-call | flops 67108864 | bytes 4194304 | tf_op jit(solution)/shard_map/pallas_call | solution.py:183
  190.7 3.3 %shard_map.96 = (f32[16,1024]{1,0:T(8,128)S(1)}, bf16[16,1024]{1,0:T(8,128)(2,1)S(1)}) custom-call(s32[16]{0:T(128)S(1)} %bitcast.32, bf16[8192,1024]{1,0:T(8,128)(2,1)} %bitcast.120, f32[1,1024]{1,0:T(1,128)S(1)} %slice.81.mask, f32[16,1024]{1,0:T(8,128)S(1)} %get-tuple-element.30.acc, bf16[1024,512]{1,0:T(8,128)(2,1)S(1)} %bitcast.16, ...), custom_call_target="tpu_custom_call" | custom-call | flops 67108864 | bytes 8388608 | tf_op jit(solution)/shard_map/pallas_call | solution.py:114
  195.3 3.5 %shard_map.97.rest_1_ = f32[16,1024]{1,0:T(8,128)S(1)} custom-call(s32[32]{0:T(128)S(1)} %copy-done.5, bf16[16,2048]{1,0:T(8,128)(2,1)S(1)} %concatenate.17.rows, f32[1,2048]{1,0:T(1,128)S(1)} %slice.82.mask, bf16[8192,1024]{1,0:T(8,128)(2,1)} %bitcast.121, bf16[8192,1024]{1,0:T(8,128)(2,1)} %bitcast.122, bf16[8192,1024]{1,0:T(8,128)(2,1)} %bitcast.123, ...), custom_call_target="tpu_custom_call" | custom-call | flops 67108864 | bytes 4194304 | tf_op jit(solution)/shard_map/pallas_call | solution.py:183
  198.8 3.3 %shard_map.98 = (f32[16,1024]{1,0:T(8,128)}, bf16[16,1024]{1,0:T(8,128)(2,1)S(1)}) custom-call(s32[16]{0:T(128)S(1)} %bitcast.33, bf16[8192,1024]{1,0:T(8,128)(2,1)} %bitcast.137, f32[1,1024]{1,0:T(1,128)S(1)} %slice.81.mask, f32[16,1024]{1,0:T(8,128)S(1)} %get-tuple-element.32.acc, bf16[1024,512]{1,0:T(8,128)(2,1)S(1)} %bitcast.17, ...), custom_call_target="tpu_custom_call" | custom-call | flops 67108864 | bytes 8388608 | tf_op jit(solution)/shard_map/pallas_call | solution.py:114
  (80 shorter events, 12.7 us)
Async XLA Ops:
  7.2 106.1 %all-gather.3.cloned.1.call-start = ((), (), s32[]{:S(2)}) async-start(), calls=%async_computation | async-start | bytes 17039360 | tf_op jit(solution)/shard_map/all_gather | solution.py:242
  9.9 113.4 %copy-start.6 = (s32[128]{0:T(128)}, s32[128]{0:T(128)S(1)}, u32[]{:S(2)}) copy-start(s32[128]{0:T(128)S(1)} %slice.74.slots) | copy-start | bytes 1540
  10.0 119.9 %copy-start.4 = (s32[32]{0:T(128)}, s32[32]{0:T(128)S(1)}, u32[]{:S(2)}) copy-start(s32[32]{0:T(128)S(1)} %slice.68.slots) | copy-start | bytes 388
  118.7 6.6 %collective-permute-start = (bf16[16,1024]{1,0:T(8,128)(2,1)S(1)}, bf16[16,1024]{1,0:T(8,128)(2,1)S(1)}, u32[]{:S(2)}, u32[]{:S(2)}) collective-permute-start(bf16[16,1024]{1,0:T(8,128)(2,1)S(1)} %get-tuple-element.20), channel_id=1, source_target_pairs={{0,64},{1,65},{2,66},{3,67},{4,68},{5,69},{6,70},{7,71},{8,72},{9,... | collective-permute-start | bytes 98312 | tf_op jit(solution)/shard_map/ppermute | solution.py:220
  119.4 6.0 %copy-start.1 = (bf16[1,1024,512]{2,1,0:T(8,128)(2,1)S(1)}, bf16[1,1024,512]{2,1,0:T(8,128)(2,1)}, u32[]{:S(2)}) copy-start(bf16[1,1024,512]{2,1,0:T(8,128)(2,1)} %param.9) | copy-start | bytes 3145732
  123.4 11.3 %collective-permute-start.2 = (bf16[16,1024]{1,0:T(8,128)(2,1)S(1)}, bf16[16,1024]{1,0:T(8,128)(2,1)S(1)}, u32[]{:S(2)}, u32[]{:S(2)}) collective-permute-start(bf16[16,1024]{1,0:T(8,128)(2,1)S(1)} %get-tuple-element.39), channel_id=1, source_target_pairs={{0,128},{1,129},{2,130},{3,131},{4,132},{5,133},{6,134},{7,135},{8... | collective-permute-start | bytes 98312 | tf_op jit(solution)/shard_map/ppermute | solution.py:220
  124.7 10.0 %collective-permute-start.3 = (bf16[16,1024]{1,0:T(8,128)(2,1)S(1)}, bf16[16,1024]{1,0:T(8,128)(2,1)S(1)}, u32[]{:S(2)}, u32[]{:S(2)}) collective-permute-start(bf16[16,1024]{1,0:T(8,128)(2,1)S(1)} %get-tuple-element.38), channel_id=1, source_target_pairs={{0,192},{1,193},{2,194},{3,195},{4,196},{5,197},{6,198},{7,199},{8... | collective-permute-start | bytes 98312 | tf_op jit(solution)/shard_map/ppermute | solution.py:220
  128.6 6.1 %collective-permute-start.1 = (bf16[16,1024]{1,0:T(8,128)(2,1)S(1)}, bf16[16,1024]{1,0:T(8,128)(2,1)S(1)}, u32[]{:S(2)}, u32[]{:S(2)}) collective-permute-start(bf16[16,1024]{1,0:T(8,128)(2,1)S(1)} %get-tuple-element.22), channel_id=1, source_target_pairs={{64,128},{65,129},{66,130},{67,131},{68,132},{69,133},{70,134},{71... | collective-permute-start | bytes 98312 | tf_op jit(solution)/shard_map/ppermute | solution.py:220
  133.8 7.0 %copy-start.9 = (s32[8,32]{1,0:T(8,128)S(1)}, s32[8,32]{1,0:T(8,128)}, u32[]{:S(2)}) copy-start(s32[8,32]{1,0:T(8,128)} %pad_add_fusion) | copy-start | bytes 3076
  133.8 7.0 %copy-start.10 = (f32[128]{0:T(128)S(1)}, f32[128]{0:T(128)}, u32[]{:S(2)}) copy-start(f32[128]{0:T(128)} %get-tuple-element.40) | copy-start | bytes 1540
  133.8 7.5 %copy-start.8 = (bf16[12,8192]{1,0:T(8,128)(2,1)S(1)}, bf16[12,8192]{1,0:T(8,128)(2,1)}, u32[]{:S(2)}) copy-start(bf16[12,8192]{1,0:T(8,128)(2,1)} %param.11) | copy-start | bytes 589828
  133.9 7.6 %copy-start.7 = (s32[128]{0:T(128)S(1)}, s32[128]{0:T(128)}, u32[]{:S(2)}) copy-start(s32[128]{0:T(128)} %copy-done.6) | copy-start | bytes 1540
  133.9 17.8 %collective-permute-start.5 = (bf16[16,1024]{1,0:T(8,128)(2,1)S(1)}, bf16[16,1024]{1,0:T(8,128)(2,1)S(1)}, u32[]{:S(2)}, u32[]{:S(2)}) collective-permute-start(bf16[16,1024]{1,0:T(8,128)(2,1)S(1)} %slice.85), channel_id=1, source_target_pairs={{64,192},{65,193},{66,194},{67,195},{68,196},{69,197},{70,198},{71... | collective-permute-start | bytes 98312 | tf_op jit(solution)/shard_map/ppermute | solution.py:220
  137.9 13.8 %collective-permute-start.4 = (bf16[16,1024]{1,0:T(8,128)(2,1)S(1)}, bf16[16,1024]{1,0:T(8,128)(2,1)S(1)}, u32[]{:S(2)}, u32[]{:S(2)}) collective-permute-start(bf16[16,1024]{1,0:T(8,128)(2,1)S(1)} %get-tuple-element.25), channel_id=1, source_target_pairs={{128,192},{129,193},{130,194},{131,195},{132,196},{133,197},{134,1... | collective-permute-start | bytes 98312 | tf_op jit(solution)/shard_map/ppermute | solution.py:220
  156.7 24.6 %collective-permute-start.11 = (bf16[16,1024]{1,0:T(8,128)(2,1)S(1)}, bf16[16,1024]{1,0:T(8,128)(2,1)S(1)}, u32[]{:S(2)}, u32[]{:S(2)}) collective-permute-start(bf16[16,1024]{1,0:T(8,128)(2,1)S(1)} %get-tuple-element.29), channel_id=1, source_target_pairs={{192,64},{193,65},{194,66},{195,67},{196,68},{197,69},{198,70},{19... | collective-permute-start | bytes 98312 | tf_op jit(solution)/shard_map/ppermute | solution.py:220
  157.4 28.4 %collective-permute-start.12 = (bf16[16,1024]{1,0:T(8,128)(2,1)S(1)}, bf16[16,1024]{1,0:T(8,128)(2,1)S(1)}, u32[]{:S(2)}, u32[]{:S(2)}) collective-permute-start(bf16[16,1024]{1,0:T(8,128)(2,1)S(1)} %get-tuple-element.29), channel_id=1, source_target_pairs={{192,0},{193,1},{194,2},{195,3},{196,4},{197,5},{198,6},{199,7},{2... | collective-permute-start | bytes 98312 | tf_op jit(solution)/shard_map/ppermute | solution.py:220
  158.1 18.5 %collective-permute-start.9 = (bf16[16,1024]{1,0:T(8,128)(2,1)S(1)}, bf16[16,1024]{1,0:T(8,128)(2,1)S(1)}, u32[]{:S(2)}, u32[]{:S(2)}) collective-permute-start(bf16[16,1024]{1,0:T(8,128)(2,1)S(1)} %get-tuple-element.29), channel_id=1, source_target_pairs={{192,128},{193,129},{194,130},{195,131},{196,132},{197,133},{198,1... | collective-permute-start | bytes 98312 | tf_op jit(solution)/shard_map/ppermute | solution.py:220
  170.9 16.3 %copy-start.5 = (s32[32]{0:T(128)S(1)}, s32[32]{0:T(128)}, u32[]{:S(2)}) copy-start(s32[32]{0:T(128)} %copy-done.4) | copy-start | bytes 388
  171.5 23.1 %collective-permute-start.6 = (bf16[12,2048]{1,0:T(8,128)(2,1)S(1)}, bf16[12,2048]{1,0:T(8,128)(2,1)S(1)}, u32[]{:S(2)}, u32[]{:S(2)}) collective-permute-start(bf16[12,2048]{1,0:T(8,128)(2,1)S(1)} %get-tuple-element.35), channel_id=1, source_target_pairs={{0,64},{64,128},{128,192},{192,0},{1,65},{65,129},{129,193},{193,1... | collective-permute-start | bytes 147464 | tf_op jit(solution)/shard_map/ppermute | solution.py:220
  176.6 18.0 %collective-permute-start.7 = (bf16[12,2048]{1,0:T(8,128)(2,1)S(1)}, bf16[12,2048]{1,0:T(8,128)(2,1)S(1)}, u32[]{:S(2)}, u32[]{:S(2)}) collective-permute-start(bf16[12,2048]{1,0:T(8,128)(2,1)S(1)} %get-tuple-element.37), channel_id=1, source_target_pairs={{0,128},{64,192},{128,0},{192,64},{1,129},{65,193},{129,1},{193,65... | collective-permute-start | bytes 147464 | tf_op jit(solution)/shard_map/ppermute | solution.py:220
  176.6 18.0 %collective-permute-start.8 = (bf16[12,2048]{1,0:T(8,128)(2,1)S(1)}, bf16[12,2048]{1,0:T(8,128)(2,1)S(1)}, u32[]{:S(2)}, u32[]{:S(2)}) collective-permute-start(bf16[12,2048]{1,0:T(8,128)(2,1)S(1)} %get-tuple-element.36), channel_id=1, source_target_pairs={{0,192},{64,0},{128,64},{192,128},{1,193},{65,1},{129,65},{193,129... | collective-permute-start | bytes 147464 | tf_op jit(solution)/shard_map/ppermute | solution.py:220
  181.3 9.3 %collective-permute-start.10 = (bf16[16,1024]{1,0:T(8,128)(2,1)S(1)}, bf16[16,1024]{1,0:T(8,128)(2,1)S(1)}, u32[]{:S(2)}, u32[]{:S(2)}) collective-permute-start(bf16[16,1024]{1,0:T(8,128)(2,1)S(1)} %get-tuple-element.31), channel_id=1, source_target_pairs={{128,64},{129,65},{130,66},{131,67},{132,68},{133,69},{134,70},{13... | collective-permute-start | bytes 98312 | tf_op jit(solution)/shard_map/ppermute | solution.py:220
  185.9 9.5 %collective-permute-start.14 = (bf16[16,1024]{1,0:T(8,128)(2,1)S(1)}, bf16[16,1024]{1,0:T(8,128)(2,1)S(1)}, u32[]{:S(2)}, u32[]{:S(2)}) collective-permute-start(bf16[16,1024]{1,0:T(8,128)(2,1)S(1)} %get-tuple-element.31), channel_id=1, source_target_pairs={{128,0},{129,1},{130,2},{131,3},{132,4},{133,5},{134,6},{135,7},{1... | collective-permute-start | bytes 98312 | tf_op jit(solution)/shard_map/ppermute | solution.py:220
  193.9 4.9 %collective-permute-start.13 = (bf16[16,1024]{1,0:T(8,128)(2,1)S(1)}, bf16[16,1024]{1,0:T(8,128)(2,1)S(1)}, u32[]{:S(2)}, u32[]{:S(2)}) collective-permute-start(bf16[16,1024]{1,0:T(8,128)(2,1)S(1)} %get-tuple-element.33), channel_id=1, source_target_pairs={{64,0},{65,1},{66,2},{67,3},{68,4},{69,5},{70,6},{71,7},{72,8},{73... | collective-permute-start | bytes 98312 | tf_op jit(solution)/shard_map/ppermute | solution.py:220
  (3 other events, 8.2 us)
Sparse Core Ops, SparseCore 0:
  10.8 102.4 all-gather.2

commit v2 on v0

v2 whole, which is shorter than its diff:
```python
import functools

import jax
import jax.numpy as jnp
from jax import lax
from jax.experimental import pallas as pl
from jax.experimental.pallas import tpu as pltpu
from jax.sharding import PartitionSpec as P

TILE = 64
GROUPS = 4
ROWS = 16
BLOCK, DEPTH = 512, 6
BF = jnp.bfloat16
F32 = jnp.float32
VMEM_LIMIT = 20 * 1024 * 1024
NT = (((1,), (1,)), ((), ()))


def mm(a, b):
    return jnp.dot(a, b, preferred_element_type=F32)


def mm_nt(a, b):
    return lax.dot_general(a, b, NT, preferred_element_type=F32)


def split_mm(product, r, w):
    high = r.astype(BF).astype(F32)
    both = product(jnp.concatenate([high, r - high], axis=0).astype(BF), w)
    return both[: r.shape[0]] + both[r.shape[0] :]


def lower_solve(residue, inverse, coupling):
    half = coupling.shape[0]
    leading = split_mm(mm, residue[:, :half], inverse[:half]).astype(BF)
    carried = residue[:, half:] - mm(leading, coupling[...])
    second = split_mm(mm, carried, inverse[half:]).astype(BF)
    return leading, second


def upper_solve(residue, inverse, coupling):
    half = coupling.shape[0]
    second = split_mm(mm_nt, residue[:, half:], inverse[half:]).astype(BF)
    carried = residue[:, :half] - mm_nt(second, coupling[...])
    return split_mm(mm_nt, carried, inverse[:half]).astype(BF), second


def store_halves(out, leading, second):
    half = leading.shape[1]
    out[:, :half] = leading.astype(out.dtype)
    out[:, half : 2 * half] = second.astype(out.dtype)


def first_kernel(acc, inverse, coupling, solved_out):
    store_halves(solved_out, *lower_solve(acc[...], inverse, coupling))


def build_kernel(places, count, targets, missing, *rest):
    pieces, solved = rest[:count], rest[count]
    near_out, message_out, tiles, sems, out_sems = rest[count + 1 :]
    width = tiles.shape[1]

    def copy(slot):
        piece, start = places[slot]
        to = pl.multiple_of(jnp.maximum(targets[slot], 0) * TILE, TILE)
        return pltpu.make_async_copy(
            pieces[piece].at[pl.ds(start, TILE)], tiles.at[pl.ds(to, TILE)], sems.at[slot]
        )

    for slot in range(len(places)):

        @pl.when(targets[slot] >= 0)
        def _(slot=slot):
            copy(slot).start()

    for i in range(tiles.shape[0] // TILE):

        @pl.when(missing[i] > 0)
        def _(i=i):
            tiles[i * TILE : (i + 1) * TILE, :] = jnp.zeros((TILE, width), BF)

    for slot in range(len(places)):

        @pl.when(targets[slot] >= 0)
        def _(slot=slot):
            copy(slot).wait()

    kept = []
    for n in range(tiles.shape[0] // width):
        part = pl.ds(n * width, width)
        kept.append(pltpu.make_async_copy(tiles.at[part], near_out.at[part], out_sems.at[n]))
        kept[-1].start()
    for n in range(tiles.shape[0] // width):
        part = slice(n * width, (n + 1) * width)
        message_out[:, part] = mm_nt(solved[...], tiles[part, :]).astype(BF)
    for copy_out in kept:
        copy_out.wait()


def in_hbm(x):
    return pltpu.with_memory_space_constraint(x, pltpu.HBM)


def build(pieces, places, targets, missing, solved):
    width = solved.shape[1]
    near_rows = missing.shape[0] * TILE
    anywhere = pl.BlockSpec(memory_space=pl.ANY)
    held = pl.BlockSpec(memory_space=pltpu.HBM)
    return pl.pallas_call(
        functools.partial(build_kernel, places, len(pieces)),
        grid_spec=pltpu.PrefetchScalarGridSpec(
            num_scalar_prefetch=2,
            grid=(1,),
            in_specs=[held] * len(pieces) + [whole(solved)],
            out_specs=[anywhere, pl.BlockSpec((ROWS, near_rows), lambda i, *_: (0, 0))],
            scratch_shapes=[
                pltpu.VMEM((near_rows, width), BF),
                pltpu.SemaphoreType.DMA((len(places),)),
                pltpu.SemaphoreType.DMA((near_rows // width,)),
            ],
        ),
        out_shape=[
            pltpu.VMEM((near_rows, width), BF),
            jax.ShapeDtypeStruct((ROWS, near_rows), BF),
        ],
        compiler_params=pltpu.CompilerParams(vmem_limit_bytes=VMEM_LIMIT),
        cost_estimate=pl.CostEstimate(
            flops=300 * width * width, bytes_accessed=15 * width * width, transcendentals=0
        ),
    )(targets, missing, *map(in_hbm, pieces), solved)


def forward_kernel(near, acc, inverse, coupling, received, acc_out, solved_out, message_out):
    width = acc.shape[1]
    residue = acc[...] - received[:, :width].astype(F32)
    acc_out[...] = residue
    store_halves(solved_out, *lower_solve(residue, inverse, coupling))
    product = mm_nt(solved_out[...], near[...])
    message_out[...] = (product + received[:, width:].astype(F32)).astype(BF)


def turn_kernel(acc, owed, inverse, coupling, received, solved_out, residue_out, message_out):
    residue = acc[...] - received[...].astype(F32)
    store_halves(solved_out, *lower_solve(residue, inverse, coupling))
    residue = solved_out[...].astype(F32) - owed[...]
    residue_out[...] = residue
    store_halves(message_out, *upper_solve(residue, inverse, coupling))


def backward_kernel(near, acc, inverse, coupling, received, acc_out, message_out):
    width = acc.shape[1]
    residue = acc[...] - mm(received[...], near[...])
    acc_out[...] = residue
    store_halves(message_out, *upper_solve(residue, inverse, coupling))
    if message_out.shape[1] > width:
        message_out[:, width:] = received[...]


def whole(x):
    return pl.BlockSpec(x.shape, lambda i, *_: (0,) * len(x.shape))


def step_call(kernel, near, chunks, operands, out_shapes):
    width = out_shapes[0].shape[1]
    specs, first = [], []
    if chunks:
        specs = [pl.BlockSpec((chunks * width, width), lambda i: (0, 0))]
        first = [pltpu.with_memory_space_constraint(near, pltpu.VMEM)]
    return pl.pallas_call(
        kernel,
        grid=(1,),
        in_specs=specs + [whole(x) for x in operands],
        out_specs=[whole(x) for x in out_shapes],
        out_shape=out_shapes,
        compiler_params=pltpu.CompilerParams(vmem_limit_bytes=VMEM_LIMIT),
        cost_estimate=pl.CostEstimate(
            flops=100 * width * width, bytes_accessed=5 * width * width, transcendentals=0
        ),
    )(*first, *operands)


def stream_kernel(blocks, count, spreading, started, rows, *rest):
    pieces, start = rest[:count], rest[count] if started else None
    out, held, sems = rest[count + started :]
    depth, height = held.shape[0], held.shape[1]

    def copy(n):
        piece, first = blocks[n]
        return pltpu.make_async_copy(
            pieces[piece].at[pl.ds(first, height)], held.at[n % depth], sems.at[n % depth]
        )

    for n in range(min(depth, len(blocks))):
        copy(n).start()
    total = start[...] if started else None
    for n in range(len(blocks)):
        copy(n).wait()
        here = slice(n * height, (n + 1) * height)
        if spreading:
            out[:, here] = mm_nt(rows[...], held[n % depth]).astype(out.dtype)
        else:
            product = mm(rows[:, here], held[n % depth])
            total = product if total is None else total + product
        if n + depth < len(blocks):
            copy(n + depth).start()
    if not spreading:
        out[...] = total


def stream(pieces, blocks, rows, spreading, start=None):
    width = pieces[0].shape[1]
    out_shape = (ROWS, len(blocks) * BLOCK) if spreading else (ROWS, width)
    inputs = [rows, *map(in_hbm, pieces)] + ([] if start is None else [start])
    specs = [pl.BlockSpec(memory_space=pltpu.HBM)] * len(pieces)
    specs = [whole(rows)] + specs + ([] if start is None else [whole(start)])
    return pl.pallas_call(
        functools.partial(
            stream_kernel, blocks, len(pieces), spreading, 0 if start is None else 1
        ),
        grid=(1,),
        in_specs=specs,
        out_specs=pl.BlockSpec(out_shape, lambda i: (0, 0)),
        out_shape=jax.ShapeDtypeStruct(out_shape, BF if spreading else F32),
        scratch_shapes=[
            pltpu.VMEM((DEPTH, BLOCK, width), BF),
            pltpu.SemaphoreType.DMA((DEPTH,)),
        ],
        compiler_params=pltpu.CompilerParams(vmem_limit_bytes=VMEM_LIMIT),
        cost_estimate=pl.CostEstimate(
            flops=32 * width * BLOCK * len(blocks),
            bytes_accessed=2 * width * BLOCK * len(blocks),
            transcendentals=0,
        ),
    )(*inputs)


def after(x, *others):
    return lax.optimization_barrier((x, *others))[0]


def body(rhs, lower_factor_tiles, tile_rows, diag_inv, inner_block, lower_row_solution):
    _, cases, width = rhs.shape
    group = lax.axis_index("grp")
    inverse, coupling = diag_inv[0], inner_block[0]
    per_panel = width // TILE
    chain_tiles = GROUPS * per_panel
    lower_tiles = lower_row_solution.shape[1] // TILE
    tile_count = chain_tiles + lower_tiles
    rows_shape = lambda dtype, panels=1: jax.ShapeDtypeStruct((ROWS, panels * width), dtype)

    def grow(x):
        return jnp.pad(x, ((0, ROWS - cases), (0, 0)))

    def hop(x, source, target):
        return lax.ppermute(x, "grp", [(source, target)])

    factor = lax.all_gather(lower_factor_tiles[0], "blk", axis=0, tiled=True)
    slot_rows = tile_rows[0, 0]
    slot_count = slot_rows.shape[0]
    places = [(0, slot * TILE) for slot in range(slot_count)]

    first = (group + 1) * per_panel
    near_tiles = (GROUPS - 1) * per_panel
    targets = jnp.where(slot_rows < chain_tiles, slot_rows - first, -1)
    numbers = jnp.arange(near_tiles, dtype=jnp.int32)
    missing = jnp.all(targets[None, :] != numbers[:, None], axis=1).astype(jnp.int32)
    low_numbers = jnp.arange(chain_tiles, tile_count, dtype=jnp.int32)
    low_numbers = jnp.roll(low_numbers.reshape(GROUPS, -1), -group, axis=0).reshape(-1)
    here = slot_rows[None, :] == low_numbers[:, None]
    slot_numbers = jnp.arange(slot_count, dtype=jnp.int32)
    turned = jnp.min(jnp.where(here, slot_numbers[None, :], slot_count), axis=1)
    low_index = jnp.where(
        (slot_rows >= chain_tiles) & (slot_rows < tile_count), slot_rows - chain_tiles, lower_tiles
    )
    low_rows = grow(lower_row_solution).reshape(ROWS, lower_tiles, TILE)
    low_rows = jnp.pad(low_rows, ((0, 0), (0, 1), (0, 0)))[:, low_index, :]
    low_rows = low_rows.reshape(ROWS, slot_count * TILE)

    acc = grow(rhs[0]).astype(F32)
    (solved,) = step_call(first_kernel, None, 0, [acc, inverse, coupling], [rows_shape(BF)])
    near, message = build([factor], places, targets, missing, solved)

    received = hop(message, 0, 1)
    blocks = [(0, n * BLOCK) for n in range(slot_count * TILE // BLOCK)]
    split = len(blocks) // 2
    owed = stream([factor], blocks[:split], low_rows[:, : split * BLOCK], False)
    for step in (1, 2):
        panels = GROUPS - 1 - step
        acc, solved, message = step_call(
            forward_kernel, near, panels, [after(acc, owed), inverse, coupling, received],
            [rows_shape(F32), rows_shape(BF), rows_shape(BF, panels)],
        )
        received = hop(message, step, step + 1)
        if step == 1:
            owed = stream([factor], blocks[split:], low_rows[:, split * BLOCK :], False, owed)
    solved, acc, message = step_call(
        turn_kernel, None, 0, [acc, owed, inverse, coupling, received],
        [rows_shape(BF), rows_shape(F32), rows_shape(BF)],
    )

    received = hop(message, 3, 2)
    beyond = [stream([factor], blocks[:split], solved, True)]
    acc, message = step_call(
        backward_kernel, near, 1, [after(acc, *beyond), inverse, coupling, received],
        [rows_shape(F32), rows_shape(BF, 2)],
    )
    received = hop(message, 2, 1)
    beyond.append(stream([factor], blocks[split:], after(solved, message), True))
    acc, message = step_call(
        backward_kernel, near, 2, [after(acc, *beyond), inverse, coupling, received],
        [rows_shape(F32), rows_shape(BF, 3)],
    )
    received = hop(message, 1, 0)
    beyond = after(jnp.concatenate(beyond, axis=1), message)[:cases].reshape(cases, slot_count, TILE)
    beyond = jnp.pad(beyond, ((0, 0), (0, 1), (0, 0)))[:, turned, :]
    beyond = beyond.reshape(cases, lower_tiles * TILE)
    beyond = after(beyond, received)
    part = lower_tiles * TILE // GROUPS
    parts = [beyond[:, :part]] + [
        lax.ppermute(
            beyond[:, shift * part : (shift + 1) * part],
            "grp",
            [(g, (g + shift) % GROUPS) for g in range(GROUPS)],
        )
        for shift in range(1, GROUPS)
    ]
    acc, settled = step_call(
        backward_kernel, near, 3, [acc, inverse, coupling, received],
        [rows_shape(F32), rows_shape(BF)],
    )
    pending = sum(p.astype(F32) for p in parts)
    return (solved[None, :cases], pending, settled[None, :cases])


def solution(mesh):
    placed = (
        P(None, "blk", "grp"),
        P(None, ("grp", "blk"), None),
        P(None, "grp", None),
        P(None, "grp", None),
        P(None, "grp", None),
        P("blk", None),
    )
    return jax.shard_map(
        body,
        mesh=mesh,
        in_specs=placed,
        out_specs=(P(None, "blk", "grp"), P("blk", "grp"), P(None, "blk", "grp")),
        check_vma=False,
    )
```

time: 1230 us -> 180 us (0.15)
  waiting for transfers between devices: 504 us -> 100 us
  blocking collectives: 345 us -> 0 us
  starting transfers between devices: 219 us -> 13.4 us
  local copies, waits for them, and re-layouts: 64.5 us -> 16 us
  matrix products: 36.2 us -> 0 us
  Pallas kernels: 0 us -> 32.7 us
  other arithmetic: 35.8 us -> 3.14 us
    while x4 -> x0, blocking collectives: 267 us -> none
    all_gather x4 -> x1, waiting for transfers between devices: 301 us -> 97 us  [body(): factor = lax.all_gather(lower_factor_tiles[0], 'blk', axis=0, tiled=True)]
    while x64 -> x0, starting transfers between devices: 184 us -> none
    ppermute x8 -> x9, waiting for transfers between devices: 113 us -> 2.4 us  [the longest x6 2.39 us: hop(): return lax.ppermute(x, 'grp', [(source, target)])]
    all_to_all x4 -> x0, blocking collectives: 78.1 us -> none  [backward_step(): lax.all_to_all(selected_rows, 'blk', split_axis=1, concat_axis=0, tiled=T...]
    all_to_all x4 -> x0, waiting for transfers between devices: 70.5 us -> none  [forward_step(): lax.all_to_all(products, 'blk', split_axis=0, concat_axis=1, tiled=True)]
    while x116 -> x0, local copies, waits for them, and re-layouts: 37.9 us -> none
    dot_general x32 -> x0, matrix products: 36.2 us -> none  [the longest x4 13.5 us: forward_step(): lax.dot_general(lax.all_gather(solved, 'blk', axis=0, tiled=True), tile_c...]
  transfers between devices with their start and end apart: 81 -> 10, of which waited for: 17 -> 4; matrix products, arithmetic and copies ran while one was open for 1% -> 5% of each run, Pallas kernels for 0% -> 11%
where the time goes in v2:
time: 180 us
  waiting for transfers between devices  100 us (56%)
  Pallas kernels  32.7 us (18%)
  local copies, waits for them, and re-layouts  16 us (9%)
  between operations  14.4 us (8%)
  starting transfers between devices  13.4 us (7%)
  other arithmetic  3.14 us (2%)
    all_gather x1, waiting for transfers between devices, body(): factor = lax.all_gather(lower_factor_tiles[0], 'blk', axis=0, tiled=True)  97 us
    pallas_call x4, Pallas kernels, stream(): pl.pallas_call(functools.partial(stream_kernel, blocks, len(pieces), spre...  16.8 us
    pallas_call x7, Pallas kernels, step_call(): pl.pallas_call(kernel, grid=(1,), in_specs=specs + [whole(x) for x in ope...  9.71 us
    unnamed x20, local copies, waits for them, and re-layouts  9.45 us
    ppermute x6, starting transfers between devices, hop(): return lax.ppermute(x, 'grp', [(source, target)])  7.9 us
    pallas_call x1, Pallas kernels, build(): pl.pallas_call(functools.partial(build_kernel, places, len(pieces)), grid...  6.16 us
    ppermute x3, starting transfers between devices, body(): lax.ppermute(beyond[:, shift * part:(shift + 1) * part], 'grp', [(g, (g +...  5.45 us
  transfers between devices with their start and end apart: 10, of which 4 were waited for; matrix products, arithmetic and copies ran while one was open for 5% of the time, Pallas kernels for 11%

profile of v2, /device:TPU:16, one launch (start us, length us, event | category | flops | bytes accessed | tf_op | source)
XLA Modules:
  0.0 179.7 jit_solution(14665079287024513193)
XLA Ops:
  13.5 1.2 copy-done.2
  14.7 1.0 copy-done.4
  16.3 97.0 %all-gather.3.cloned.1.call-done = bf16[1,8192,1024]{2,1,0:T(8,128)(2,1)} async-done(((bf16[1,128,1024]{2,1,0:T(8,128)(2,1)}), bf16[1,8192,1024]{2,1,0:T(8,128)(2,1)}) %all-gather.3.cloned.1.call-update) | async-done | bytes 16777232 | tf_op jit(solution)/shard_map/all_gather | solution.py:258
  113.3 6.2 %shard_map.86 = (bf16[3072,1024]{1,0:T(8,128)(2,1)S(1)}, bf16[16,3072]{1,0:T(8,128)(2,1)}) custom-call(s32[128]{0:T(128)S(1)} %compare_select_fusion.2.targets, s32[48]{0:T(128)S(1)} %convert_element_type.26.missing, bf16[8192,1024]{1,0:T(8,128)(2,1)} %bitcast.37, bf16[16,1024]{1,0:T(8,128)(2,1)S(1)} %shard_map.85.rest_1_), custom_call_target="tpu_custom_call" | custom-call | flops 314572800 | bytes 15728640 | tf_op jit(solution)/shard_map/pallas_call | solution.py:110
  119.5 2.6 %copy-done = bf16[3072,1024]{1,0:T(8,128)(2,1)} copy-done((bf16[3072,1024]{1,0:T(8,128)(2,1)}, bf16[3072,1024]{1,0:T(8,128)(2,1)S(1)}, u32[]{:S(2)}) %copy-start) | copy-done | bytes 6291480
  122.1 1.4 collective-permute-start
  123.6 4.1 %shard_map.87.rest_1_ = f32[16,1024]{1,0:T(8,128)S(1)} custom-call(bf16[16,4096]{1,0:T(8,128)(2,1)S(1)} %get-tuple-element.49.rows, bf16[8192,1024]{1,0:T(8,128)(2,1)} %bitcast.38), custom_call_target="tpu_custom_call" | custom-call | flops 134217728 | bytes 8388608 | tf_op jit(solution)/shard_map/pallas_call | solution.py:217
  128.5 3.0 %shard_map.88 = (f32[16,1024]{1,0:T(8,128)S(1)}, bf16[16,1024]{1,0:T(8,128)(2,1)}, bf16[16,2048]{1,0:T(8,128)(2,1)S(1)}) custom-call(bf16[3072,1024]{1,0:T(8,128)(2,1)S(1)} %bitcast.22, f32[16,1024]{1,0:T(8,128)S(1)} %pad_convert_fusion.acc, bf16[1024,512]{1,0:T(8,128)(2,1)S(1)} %bitcast.24, bf16[512,512]{1,0:T(8,128)(2,1)S(1)} %bitcast.31, ...), custom_call_target="tpu_custom_call" | custom-call | flops 104857600 | bytes 5242880 | tf_op jit(solution)/shard_map/pallas_call | solution.py:170
  131.4 1.3 collective-permute-start.1
  132.9 3.9 %shard_map.89.owed = f32[16,1024]{1,0:T(8,128)S(1)} custom-call(bf16[16,4096]{1,0:T(8,128)(2,1)S(1)} %get-tuple-element.48.rows, bf16[8192,1024]{1,0:T(8,128)(2,1)} %bitcast.39, f32[16,1024]{1,0:T(8,128)S(1)} %shard_map.87.rest_1_), custom_call_target="tpu_custom_call" | custom-call | flops 134217728 | bytes 8388608 | tf_op jit(solution)/shard_map/pallas_call | solution.py:217
  137.6 1.5 shard_map.90
  139.1 1.7 collective-permute-start.2
  140.8 1.6 collective-permute-done.2.received
  142.3 1.1 shard_map.91
  143.4 1.3 collective-permute-start.3
  144.7 4.4 %shard_map.92 = bf16[16,4096]{1,0:T(8,128)(2,1)S(1)} custom-call(bf16[16,1024]{1,0:T(8,128)(2,1)S(1)} %get-tuple-element.37.rows, bf16[8192,1024]{1,0:T(8,128)(2,1)} %bitcast.40), custom_call_target="tpu_custom_call" | custom-call | flops 134217728 | bytes 8388608 | tf_op jit(solution)/shard_map/pallas_call | solution.py:217
  150.2 1.5 collective-permute-start.4
  152.3 4.4 %shard_map.94 = bf16[16,4096]{1,0:T(8,128)(2,1)S(1)} custom-call(bf16[16,1024]{1,0:T(8,128)(2,1)S(1)} %get-tuple-element.37.rows, bf16[8192,1024]{1,0:T(8,128)(2,1)} %bitcast.41), custom_call_target="tpu_custom_call" | custom-call | flops 134217728 | bytes 8388608 | tf_op jit(solution)/shard_map/pallas_call | solution.py:217
  156.7 1.2 shard_map.95
  160.6 2.0 %collective-permute-start.6 = (bf16[12,2048]{1,0:T(8,128)(2,1)S(1)}, bf16[12,2048]{1,0:T(8,128)(2,1)S(1)}, u32[]{:S(2)}, u32[]{:S(2)}) collective-permute-start(bf16[12,2048]{1,0:T(8,128)(2,1)S(1)} %get-tuple-element.45), channel_id=1, source_target_pairs={{0,64},{64,128},{128,192},{192,0},{1,65},{65,129},{129,193},{193,1... | collective-permute-start | bytes 147464 | tf_op jit(solution)/shard_map/ppermute | solution.py:321
  162.7 3.4 %collective-permute-start.7 = (bf16[12,2048]{1,0:T(8,128)(2,1)S(1)}, bf16[12,2048]{1,0:T(8,128)(2,1)S(1)}, u32[]{:S(2)}, u32[]{:S(2)}) collective-permute-start(bf16[12,2048]{1,0:T(8,128)(2,1)S(1)} %get-tuple-element.47), channel_id=1, source_target_pairs={{0,128},{64,192},{128,0},{192,64},{1,129},{65,193},{129,1},{193,65... | collective-permute-start | bytes 147464 | tf_op jit(solution)/shard_map/ppermute | solution.py:321
  166.1 2.8 %copy-done.1 = bf16[3072,1024]{1,0:T(8,128)(2,1)S(1)} copy-done((bf16[3072,1024]{1,0:T(8,128)(2,1)S(1)}, bf16[3072,1024]{1,0:T(8,128)(2,1)}, u32[]{:S(2)}) %copy-start.1) | copy-done | bytes 6291480
  168.9 1.0 copy-done.6
  169.9 1.6 shard_map.96
  (62 shorter events, 14.2 us)
Async XLA Ops:
  7.2 106.1 %all-gather.3.cloned.1.call-start = ((), (), s32[]{:S(2)}) async-start(), calls=%async_computation | async-start | bytes 17039360 | tf_op jit(solution)/shard_map/all_gather | solution.py:258
  13.5 1.2 copy-start.2
  14.7 1.0 copy-start.4
  113.3 14.4 %copy-start.3 = (bf16[1,1024,512]{2,1,0:T(8,128)(2,1)S(1)}, bf16[1,1024,512]{2,1,0:T(8,128)(2,1)}, u32[]{:S(2)}) copy-start(bf16[1,1024,512]{2,1,0:T(8,128)(2,1)} %param.9) | copy-start | bytes 3145732
  113.3 19.4 %copy-start.7 = (s32[1,1,128]{2,1,0:T(1,128)S(1)}, s32[1,1,128]{2,1,0:T(1,128)}, u32[]{:S(2)}) copy-start(s32[1,1,128]{2,1,0:T(1,128)} %param.8) | copy-start | bytes 1540
  119.5 2.6 %copy-start = (bf16[3072,1024]{1,0:T(8,128)(2,1)}, bf16[3072,1024]{1,0:T(8,128)(2,1)S(1)}, u32[]{:S(2)}) copy-start(bf16[3072,1024]{1,0:T(8,128)(2,1)S(1)} %get-tuple-element.24.near) | copy-start | bytes 18874372
  122.1 5.6 %slice-start = ((s8[6291456]{0:T(1024)(128)(4,1)}), s8[2097152]{0:T(1024)(128)(4,1)S(1)}, s32[]{:S(2)}) async-start(s8[6291456]{0:T(1024)(128)(4,1)} %bitcast.21), calls=%async_computation.1 | async-start | bytes 4194304
  122.1 5.6 %collective-permute-start = (bf16[16,3072]{1,0:T(8,128)(2,1)}, bf16[16,3072]{1,0:T(8,128)(2,1)}, u32[]{:S(2)}, u32[]{:S(2)}) collective-permute-start(bf16[16,3072]{1,0:T(8,128)(2,1)} %get-tuple-element.26), channel_id=1, source_target_pairs={{0,64},{1,65},{2,66},{3,67},{4,68},{5,69},{6,70},{7,71},{8,72},{9,... | collective-permute-start | bytes 294920 | tf_op jit(solution)/shard_map/ppermute | solution.py:256
  123.6 4.1 %copy-start.5 = (bf16[1,512,512]{2,1,0:T(8,128)(2,1)S(1)}, bf16[1,512,512]{2,1,0:T(8,128)(2,1)}, u32[]{:S(2)}) copy-start(bf16[1,512,512]{2,1,0:T(8,128)(2,1)} %param.10) | copy-start | bytes 1572868
  123.6 4.8 %slice-start.1 = ((s8[6291456]{0:T(1024)(128)(4,1)}), s8[4194304]{0:T(1024)(128)(4,1)S(1)}, s32[]{:S(2)}) async-start(s8[6291456]{0:T(1024)(128)(4,1)} %bitcast.21), calls=%async_computation.2 | async-start | bytes 8388608
  131.4 6.1 %collective-permute-start.1 = (bf16[16,2048]{1,0:T(8,128)(2,1)S(1)}, bf16[16,2048]{1,0:T(8,128)(2,1)S(1)}, u32[]{:S(2)}, u32[]{:S(2)}) collective-permute-start(bf16[16,2048]{1,0:T(8,128)(2,1)S(1)} %get-tuple-element.29), channel_id=1, source_target_pairs={{64,128},{65,129},{66,130},{67,131},{68,132},{69,133},{70,134},{71... | collective-permute-start | bytes 196616 | tf_op jit(solution)/shard_map/ppermute | solution.py:256
  139.1 3.3 %collective-permute-start.2 = (bf16[16,1024]{1,0:T(8,128)(2,1)S(1)}, bf16[16,1024]{1,0:T(8,128)(2,1)S(1)}, u32[]{:S(2)}, u32[]{:S(2)}) collective-permute-start(bf16[16,1024]{1,0:T(8,128)(2,1)S(1)} %get-tuple-element.31), channel_id=1, source_target_pairs={{128,192},{129,193},{130,194},{131,195},{132,196},{133,197},{134,1... | collective-permute-start | bytes 98312 | tf_op jit(solution)/shard_map/ppermute | solution.py:256
  143.4 5.8 %collective-permute-start.3 = (bf16[16,1024]{1,0:T(8,128)(2,1)S(1)}, bf16[16,1024]{1,0:T(8,128)(2,1)S(1)}, u32[]{:S(2)}, u32[]{:S(2)}) collective-permute-start(bf16[16,1024]{1,0:T(8,128)(2,1)S(1)} %get-tuple-element.35), channel_id=1, source_target_pairs={{192,128},{193,129},{194,130},{195,131},{196,132},{197,133},{198,1... | collective-permute-start | bytes 98312 | tf_op jit(solution)/shard_map/ppermute | solution.py:256
  150.2 6.5 %collective-permute-start.4 = (bf16[16,2048]{1,0:T(8,128)(2,1)S(1)}, bf16[16,2048]{1,0:T(8,128)(2,1)S(1)}, u32[]{:S(2)}, u32[]{:S(2)}) collective-permute-start(bf16[16,2048]{1,0:T(8,128)(2,1)S(1)} %get-tuple-element.36), channel_id=1, source_target_pairs={{128,64},{129,65},{130,66},{131,67},{132,68},{133,69},{134,70},{13... | collective-permute-start | bytes 196616 | tf_op jit(solution)/shard_map/ppermute | solution.py:256
  157.9 2.7 %collective-permute-start.5 = (bf16[16,3072]{1,0:T(8,128)(2,1)S(1)}, bf16[16,3072]{1,0:T(8,128)(2,1)S(1)}, u32[]{:S(2)}, u32[]{:S(2)}) collective-permute-start(bf16[16,3072]{1,0:T(8,128)(2,1)S(1)} %get-tuple-element.40), channel_id=1, source_target_pairs={{64,0},{65,1},{66,2},{67,3},{68,4},{69,5},{70,6},{71,7},{72,8},{73... | collective-permute-start | bytes 294920 | tf_op jit(solution)/shard_map/ppermute | solution.py:256
  160.6 11.5 %collective-permute-start.6 = (bf16[12,2048]{1,0:T(8,128)(2,1)S(1)}, bf16[12,2048]{1,0:T(8,128)(2,1)S(1)}, u32[]{:S(2)}, u32[]{:S(2)}) collective-permute-start(bf16[12,2048]{1,0:T(8,128)(2,1)S(1)} %get-tuple-element.45), channel_id=1, source_target_pairs={{0,64},{64,128},{128,192},{192,0},{1,65},{65,129},{129,193},{193,1... | collective-permute-start | bytes 147464 | tf_op jit(solution)/shard_map/ppermute | solution.py:321
  162.7 9.5 %collective-permute-start.8 = (bf16[12,2048]{1,0:T(8,128)(2,1)S(1)}, bf16[12,2048]{1,0:T(8,128)(2,1)S(1)}, u32[]{:S(2)}, u32[]{:S(2)}) collective-permute-start(bf16[12,2048]{1,0:T(8,128)(2,1)S(1)} %get-tuple-element.46), channel_id=1, source_target_pairs={{0,192},{64,0},{128,64},{192,128},{1,193},{65,1},{129,65},{193,129... | collective-permute-start | bytes 147464 | tf_op jit(solution)/shard_map/ppermute | solution.py:321
  162.7 9.4 %collective-permute-start.7 = (bf16[12,2048]{1,0:T(8,128)(2,1)S(1)}, bf16[12,2048]{1,0:T(8,128)(2,1)S(1)}, u32[]{:S(2)}, u32[]{:S(2)}) collective-permute-start(bf16[12,2048]{1,0:T(8,128)(2,1)S(1)} %get-tuple-element.47), channel_id=1, source_target_pairs={{0,128},{64,192},{128,0},{192,64},{1,129},{65,193},{129,1},{193,65... | collective-permute-start | bytes 147464 | tf_op jit(solution)/shard_map/ppermute | solution.py:321
  166.1 2.8 %copy-start.1 = (bf16[3072,1024]{1,0:T(8,128)(2,1)S(1)}, bf16[3072,1024]{1,0:T(8,128)(2,1)}, u32[]{:S(2)}) copy-start(bf16[3072,1024]{1,0:T(8,128)(2,1)} %copy-done) | copy-start | bytes 18874372
  168.9 1.0 copy-start.6
Sparse Core Ops, SparseCore 0:
  10.8 102.4 all-gather.2
